TPU v7x, 512 devices: a whole 4x4x16 slice. The times are simulated.
512 devices in a mesh: space: 32 (over x, z_lo, core), vel: 16 (over z_hi, y).
Axes of the slice: x: 4, y: 4, z: 16 (z_hi: 4, z_lo: 4; z = z_hi * 4 + z_lo), core: 2. Of those that a mesh axis runs over, the one named last changes fastest.
Arguments:
- distribution: float32 [512, 48, 2304], P('space', 'vel'), may hold values from 0 to 5.4, as said below
- freestream: float32 [48, 2304], P('vel'), may hold values from 0 to 3, as said below
- face_area: float32 [3, 6, 512], P(None, None, 'space'), may hold values from -2.5 to 2.5
- cell_volume: float32 [512], P('space'), may hold values from 1 to 3
- neighbours: int32 [6, 512], P(None, 'space'), may hold values from 0 to 23
- wall_flags: int32 [6, 512], P(None, 'space'), may hold values 0 or 1
- send_cells: int32 [2, 128], P(None, 'space'), may hold values from 0 to 15, as said below
Outputs:
- new_distribution: float32 [512, 48, 2304], P('space', 'vel')
Inputs may be any that keep to these rules, and one draw needn't show every extreme that they name: `distribution`: smooth in no direction; nonnegative, with a positive sum over velocities in every cell. `freestream`: nonnegative. `send_cells`: a local cell index of the sending block; distinct within each row of one block. `neighbours`: rows below 16 are the block's own cells, then 4 rows from the block below, then 4 from the block above; unused where the face is a wall.
All inputs are finite; a program needn't handle non-finite values. No bound on the sum of `wall_flags` on one device may be relied on, other than what follows from the above.
Results may differ from a plain program's by a relative error of at most 0.0003.
Values sent between devices are 32-bit elements; how exact they have to be, the bound alone decides.
A program may use at most 64 MiB of HBM per device.

v0:
```python
import jax
import jax.numpy as jnp
from jax import lax
from jax.sharding import PartitionSpec as P

NV = 48
SUBSTEPS = 2


GRID_STEP = 0.25
TIME_STEP = 0.02
WALL_TEMP = 1.0
COLLISION_SCALE = 0.002
MU_POWER_LAW = 0.81
ANISO_MIX_WEIGHT = 0.5


def from_behind(value, axis, steps):
    count = lax.axis_size(axis)
    first, last = (max(0, -steps), min(count, count - steps))
    return lax.ppermute(value, axis, [(source, source + steps) for source in range(first, last)])


def padded_2(cells, sides, width):
    for axis, dim in sides:
        count = lax.axis_size(axis)
        ends = count - 1
        head = lax.slice_in_dim(cells, 0, width, axis=dim)
        tail = lax.slice_in_dim(cells, cells.shape[dim] - width, cells.shape[dim], axis=dim)
        cells = jnp.concatenate(
            [
                lax.ppermute(tail, axis, [(i, (i + 1) % count) for i in range(ends)]),
                cells,
                lax.ppermute(head, axis, [((i + 1) % count, i) for i in range(ends)]),
            ],
            axis=dim,
        )
    return cells


def grid_axis(points, first_point):
    return ((jnp.arange(points) + first_point).astype(jnp.float32) - (NV - 1) / 2.0) * GRID_STEP


def plane_axes():
    grid_line = grid_axis(NV, 0)
    return (jnp.repeat(grid_line, NV), jnp.tile(grid_line, NV))


def moment_weights(plane_vel, grid_y, grid_z):
    unity_grid = jnp.ones((plane_vel.shape[0], grid_y.shape[0]), jnp.float32)
    vel_x = plane_vel[:, None] * unity_grid
    vel_y = grid_y[None, :] * unity_grid
    vel_z = grid_z[None, :] * unity_grid
    return jnp.stack(
        [
            unity_grid,
            vel_x,
            vel_y,
            vel_z,
            vel_x * vel_x,
            vel_y * vel_y,
            vel_z * vel_z,
            vel_x * vel_y,
            vel_x * vel_z,
            vel_y * vel_z,
        ]
    )


def moment_sums(values, weights):
    return jnp.einsum("cxj,mxj->mc", values, weights, precision=lax.Precision.HIGHEST)


def per_cell(values):
    return values[:, None, None]


def shift_flat(values, offset):
    filler = jnp.zeros(values.shape[:-1] + (abs(offset),), values.dtype)
    if offset > 0:
        return jnp.concatenate([values[..., offset:], filler], axis=-1)
    return jnp.concatenate([filler, values[..., :offset]], axis=-1)


def fp_update(padded, plane_ext, grid_y, grid_z, moments_sum):
    flat_size = padded.shape[-1]
    z_index = jnp.arange(flat_size) % NV
    keep_up = (z_index < NV - 1).astype(padded.dtype)
    keep_down = (z_index > 0).astype(padded.dtype)

    def along_y(values, offset):
        return shift_flat(values, offset * NV)

    def along_z(values, offset):
        return shift_flat(values, offset) * (keep_up if offset > 0 else keep_down)

    mass_sum = moments_sum[0]
    particle_concentration = GRID_STEP**3 * mass_sum
    mean_x = moments_sum[1] / mass_sum
    mean_y = moments_sum[2] / mass_sum
    mean_z = moments_sum[3] / mass_sum
    second_moment_horizontal = moments_sum[4] / mass_sum - mean_x * mean_x
    second_moment_lateral = moments_sum[5] / mass_sum - mean_y * mean_y
    second_moment_vertical = moments_sum[6] / mass_sum - mean_z * mean_z
    cov_xy = moments_sum[7] / mass_sum - mean_x * mean_y
    cov_xz = moments_sum[8] / mass_sum - mean_x * mean_z
    cov_yz = moments_sum[9] / mass_sum - mean_y * mean_z
    kinetic_heat_level = (
        second_moment_horizontal + second_moment_lateral + second_moment_vertical
    ) / 3.0
    collision_frequency = (
        COLLISION_SCALE * particle_concentration * kinetic_heat_level ** (1.0 - MU_POWER_LAW)
    )
    centre = padded[:, 1:-1]
    next_plane = padded[:, 2:]
    prev_plane = padded[:, :-2]
    drift_x = (plane_ext[2:][None, :, None] - per_cell(mean_x)) * next_plane - (
        plane_ext[:-2][None, :, None] - per_cell(mean_x)
    ) * prev_plane
    flow_y = (grid_y[None, None, :] - per_cell(mean_y)) * centre
    drift_y = along_y(flow_y, 1) - along_y(flow_y, -1)
    flow_z = (grid_z[None, None, :] - per_cell(mean_z)) * centre
    drift_z = along_z(flow_z, 1) - along_z(flow_z, -1)
    drift = (drift_x + drift_y + drift_z) / (2.0 * GRID_STEP)
    doubled = 2.0 * centre
    second_xx = next_plane - doubled + prev_plane
    up_y = along_y(centre, 1)
    down_y = along_y(centre, -1)
    second_yy = up_y + down_y - doubled
    second_zz = along_z(centre, 1) + along_z(centre, -1) - doubled
    second_xy = (
        along_y(next_plane, 1)
        - along_y(next_plane, -1)
        - along_y(prev_plane, 1)
        + along_y(prev_plane, -1)
    ) / 4.0
    second_xz = (
        along_z(next_plane, 1)
        - along_z(next_plane, -1)
        - along_z(prev_plane, 1)
        + along_z(prev_plane, -1)
    ) / 4.0
    second_yz = (
        along_z(up_y, 1) - along_z(up_y, -1) - along_z(down_y, 1) + along_z(down_y, -1)
    ) / 4.0
    spherical_share = (1.0 - ANISO_MIX_WEIGHT) * kinetic_heat_level
    diffusion = (
        per_cell(spherical_share + ANISO_MIX_WEIGHT * second_moment_horizontal) * second_xx
        + per_cell(spherical_share + ANISO_MIX_WEIGHT * second_moment_lateral) * second_yy
        + per_cell(spherical_share + ANISO_MIX_WEIGHT * second_moment_vertical) * second_zz
        + 2.0
        * ANISO_MIX_WEIGHT
        * (
            per_cell(cov_xy) * second_xy
            + per_cell(cov_xz) * second_xz
            + per_cell(cov_yz) * second_yz
        )
    )
    return centre + per_cell(collision_frequency) * (drift + diffusion / (GRID_STEP * GRID_STEP))


def body(distribution, freestream, face_area, cell_volume, neighbours, wall_flags, send_cells):
    cell_count, planes, flat_size = distribution.shape
    halo_count = send_cells.shape[1]
    faces = face_area.shape[1]
    vel_index = lax.axis_index("vel")
    blocks = lax.axis_size("space")
    space_index = lax.axis_index("space")
    grid_y, grid_z = plane_axes()
    first_plane = vel_index * planes
    plane_vel = grid_axis(planes, first_plane)
    maxwell = jnp.exp(
        -(plane_vel[:, None] ** 2 + grid_y[None, :] ** 2 + grid_z[None, :] ** 2) / (2.0 * WALL_TEMP)
    )
    received = []
    for side_row, offset in ((1, 1), (0, -1)):
        picked = distribution[send_cells[side_row]]
        received.append(from_behind(picked, "space", offset))
    normals = []
    out_list = []
    in_list = []
    for face_slot in range(faces):
        normal_vel = (
            per_cell(face_area[0, face_slot]) * plane_vel[None, :, None]
            + per_cell(face_area[1, face_slot]) * grid_y[None, None, :]
            + per_cell(face_area[2, face_slot]) * grid_z[None, None, :]
        )
        normals.append(normal_vel)
        out_list.append(
            jnp.sum(jnp.maximum(normal_vel, 0.0) * distribution, axis=(1, 2)) * GRID_STEP**3
        )
        in_list.append(
            jnp.sum(jnp.maximum(-normal_vel, 0.0) * maxwell[None], axis=(1, 2)) * GRID_STEP**3
        )
    totals = lax.psum((jnp.stack(out_list), jnp.stack(in_list)), "vel")
    wall_ratio = totals[0] / totals[1]
    far_field = jnp.broadcast_to(freestream, (halo_count, planes, flat_size))
    below_rows = jnp.where(space_index == 0, far_field, received[0])
    above_rows = jnp.where(space_index == blocks - 1, far_field, received[1])
    extended = jnp.concatenate([distribution, below_rows, above_rows], axis=0)
    flux_sum = jnp.zeros_like(distribution)
    for face_slot in range(faces):
        normal_vel = normals[face_slot]
        wall_in = per_cell(wall_ratio[face_slot]) * maxwell[None]
        upwind_side = jnp.where(
            per_cell(wall_flags[face_slot]) == 1, wall_in, extended[neighbours[face_slot]]
        )
        flux_sum = (
            flux_sum
            + jnp.maximum(normal_vel, 0.0) * distribution
            + jnp.minimum(normal_vel, 0.0) * upwind_side
        )
    moved = distribution - TIME_STEP * flux_sum / per_cell(cell_volume)
    weights = moment_weights(plane_vel, grid_y, grid_z)
    plane_ext = grid_axis(planes + 2, first_plane - 1)
    for substep in range(SUBSTEPS):
        moments_sum = lax.psum(moment_sums(moved, weights), "vel")
        padded = padded_2(moved, (("vel", 1),), 1)
        moved = fp_update(padded, plane_ext, grid_y, grid_z, moments_sum)
    return moved


def solution(mesh):
    in_specs = (
        P("space", "vel", None),
        P("vel", None),
        P(None, None, "space"),
        P("space"),
        P(None, "space"),
        P(None, "space"),
        P(None, "space"),
    )
    out_specs = P("space", "vel", None)
    return jax.shard_map(body, mesh=mesh, in_specs=in_specs, out_specs=out_specs, check_vma=False)
```

profile of v0, /device:TPU:422, one launch (start us, length us, event | category | flops | bytes accessed | tf_op | source)
XLA Modules:
  0.0 244.1 jit_solution(5226614514190608168)
XLA Ops:
  0.0 0.8 fusion.58
  0.8 1.9 gather_fusion.1
  2.7 2.4 collective-permute-start.1
  5.1 0.8 gather_fusion
  5.9 2.0 collective-permute-start
  11.1 1.9 fusion.42
  13.2 2.0 multiply_reduce_fusion
  15.4 52.9 %all-reduce.40 = (f32[6,16]{1,0:T(8,128)S(1)}, f32[6,16]{1,0:T(8,128)S(1)}) all-reduce(f32[6,16]{1,0:T(8,128)S(1)} %stack.48, f32[6,16]{1,0:T(8,128)S(1)} %stack.49), channel_id=1, replica_groups=mesh['space'=32,'vel'=16] {'vel'}, use_global_device_ids=true, to_apply=%region_6.0 | all-reduce | flops 192 | bytes 1536 | tf_op jit(solution)/shard_map/psum | solution.py:196
  71.3 0.9 gather_fusion.7
  72.2 0.9 gather_fusion.6
  73.1 1.0 gather_fusion.5
  74.2 1.8 gather_fusion.4
  76.0 1.8 gather_fusion.3
  77.8 1.7 gather_fusion.2
  80.3 5.8 %copy_subtract_fusion = f32[16,3,2304]{2,1,0:T(4,128)S(1)} fusion(f32[16,3,2304]{2,0,1:T(8,128)S(1)} %copy-done, f32[16,3,2304]{2,1,0:T(4,128)S(1)} %gather_fusion.7, f32[16,3,2304]{2,1,0:T(4,128)S(1)} %gather_fusion.6, f32[16,3,2304]{2,1,0:T(4,128)S(1)} %gather_fusion.5, f32[16,3,2304]{2,1,0:T(4,128)} %gather_fusion.4, f32[16,3,2304]{2,1,0:T(4,128)} %gather_fusion.3, ...), kind=kLoop, calls=%fused_computation.33 | loop fusion | flops 6856704 | bytes 5337760 | tf_op jit(solution)/shard_map/sub | solution.py:214
  86.3 0.7 convolution_bitcast_fusion.1
  87.1 47.9 %psum.30 = f32[10,16]{1,0:T(8,128)S(1)} all-reduce(f32[10,16]{1,0:T(8,128)S(1)} %convolution_bitcast_fusion.1), channel_id=1, replica_groups=mesh['space'=32,'vel'=16] {'vel'}, use_global_device_ids=true, to_apply=%region_14.15 | all-reduce | flops 160 | bytes 1280 | tf_op jit(solution)/shard_map/psum | solution.py:218
  135.1 3.1 %collective-permute-start.2 = (f32[16,1,2304]{2,1,0:T(1,128)S(1)}, f32[16,1,2304]{2,1,0:T(1,128)S(1)}, u32[]{:S(2)}, u32[]{:S(2)}) collective-permute-start(f32[16,1,2304]{2,1,0:T(1,128)S(1)} %get-tuple-element.81), channel_id=1, source_target_pairs={{1,0},{2,1},{3,2},{4,3},{5,4},{6,5},{7,6},{8,7},{9,8},{10,9},{11,1... | collective-permute-start | bytes 442376 | tf_op jit(solution)/shard_map/ppermute | solution.py:34
  138.3 2.9 %collective-permute-start.3 = (f32[16,1,2304]{2,1,0:T(1,128)S(1)}, f32[16,1,2304]{2,1,0:T(1,128)S(1)}, u32[]{:S(2)}, u32[]{:S(2)}) collective-permute-start(f32[16,1,2304]{2,1,0:T(1,128)S(1)} %get-tuple-element.82), channel_id=1, source_target_pairs={{0,1},{1,2},{2,3},{3,4},{4,5},{5,6},{6,7},{7,8},{8,9},{9,10},{10,1... | collective-permute-start | bytes 442376 | tf_op jit(solution)/shard_map/ppermute | solution.py:32
  143.0 1.1 collective-permute-done.2
  144.1 11.9 %collective-permute-done.3 = f32[16,1,2304]{2,1,0:T(1,128)S(1)} collective-permute-done((f32[16,1,2304]{2,1,0:T(1,128)S(1)}, f32[16,1,2304]{2,1,0:T(1,128)S(1)}, u32[]{:S(2)}, u32[]{:S(2)}) %collective-permute-start.3) | collective-permute-done | bytes 147488 | tf_op jit(solution)/shard_map/ppermute | solution.py:32
  156.1 2.2 fusion.14
  159.4 1.7 fusion.90
  161.8 4.6 %multiply_add_fusion.1 = f32[16,3,2304]{2,1,0:T(4,128)S(1)} fusion(f32[16,3,2304]{2,1,0:T(4,128)S(1)} %copy_subtract_fusion, f32[16,1,2304]{2,1,0:T(1,128)S(1)} %collective-permute-done.3, f32[16,1,2304]{2,1,0:T(1,128)S(1)} %collective-permute-done.2, f32[16,3,2303]{2,1,0:T(4,128)S(1)} %get-tuple-element.80, f32[16,3,2303]{2,1,0:T(4,128)S(1)} %get-tuple-element.79, ...), kind=kLoop, calls=%fused_computation.81 | loop fusion | flops 6635520 | bytes 9085888 | tf_op jit(solution)/shard_map/add | solution.py:160
  167.1 47.7 %psum.31 = f32[10,16]{1,0:T(8,128)S(1)} all-reduce(f32[10,16]{1,0:T(8,128)S(1)} %convolution_bitcast_fusion), channel_id=1, replica_groups=mesh['space'=32,'vel'=16] {'vel'}, use_global_device_ids=true, to_apply=%region_15.16 | all-reduce | flops 160 | bytes 1280 | tf_op jit(solution)/shard_map/psum | solution.py:218
  215.4 3.1 %collective-permute-start.4 = (f32[16,1,2304]{2,1,0:T(1,128)S(1)}, f32[16,1,2304]{2,1,0:T(1,128)S(1)}, u32[]{:S(2)}, u32[]{:S(2)}) collective-permute-start(f32[16,1,2304]{2,1,0:T(1,128)S(1)} %get-tuple-element.61), channel_id=1, source_target_pairs={{1,0},{2,1},{3,2},{4,3},{5,4},{6,5},{7,6},{8,7},{9,8},{10,9},{11,1... | collective-permute-start | bytes 442376 | tf_op jit(solution)/shard_map/ppermute | solution.py:34
  218.5 2.9 %collective-permute-start.5 = (f32[16,1,2304]{2,1,0:T(1,128)S(1)}, f32[16,1,2304]{2,1,0:T(1,128)S(1)}, u32[]{:S(2)}, u32[]{:S(2)}) collective-permute-start(f32[16,1,2304]{2,1,0:T(1,128)S(1)} %get-tuple-element.62), channel_id=1, source_target_pairs={{0,1},{1,2},{2,3},{3,4},{4,5},{5,6},{6,7},{7,8},{8,9},{9,10},{10,1... | collective-permute-start | bytes 442376 | tf_op jit(solution)/shard_map/ppermute | solution.py:32
  222.5 11.0 %collective-permute-done.5 = f32[16,1,2304]{2,1,0:T(1,128)S(1)} collective-permute-done((f32[16,1,2304]{2,1,0:T(1,128)S(1)}, f32[16,1,2304]{2,1,0:T(1,128)S(1)}, u32[]{:S(2)}, u32[]{:S(2)}) %collective-permute-start.5) | collective-permute-done | bytes 147488 | tf_op jit(solution)/shard_map/ppermute | solution.py:32
  233.6 2.2 fusion.6
  236.9 1.7 fusion.86
  238.6 4.7 %multiply_add_fusion = f32[16,3,2304]{2,1,0:T(4,128)S(1)} fusion(f32[16,3,2304]{2,1,0:T(4,128)S(1)} %multiply_add_fusion.1, f32[16,1,2304]{2,1,0:T(1,128)S(1)} %collective-permute-done.5, f32[16,1,2304]{2,1,0:T(1,128)S(1)} %collective-permute-done.4, f32[16,3,2303]{2,1,0:T(4,128)S(1)} %get-tuple-element.60, f32[16,3,2303]{2,1,0:T(4,128)S(1)} %get-tuple-element.59, ...), kind=kLoop, calls=%fused_computation.77 | loop fusion | flops 6635520 | bytes 9085888 | tf_op jit(solution)/shard_map/add | solution.py:160
  243.3 0.8 copy.20
  (169 shorter events, 14.1 us)
Async XLA Ops:
  0.8 4.3 %copy-start = (f32[16,3,2304]{2,0,1:T(8,128)S(1)}, f32[16,3,2304]{2,0,1:T(8,128)}, u32[]{:S(2)}) copy-start(f32[16,3,2304]{2,0,1:T(8,128)} %param.7) | copy-start | bytes 1327108
  2.7 68.2 %collective-permute-start.1 = (f32[4,3,2304]{2,0,1:T(4,128)S(1)}, f32[4,3,2304]{2,0,1:T(4,128)S(1)}, u32[]{:S(2)}, u32[]{:S(2)}) collective-permute-start(f32[4,3,2304]{2,0,1:T(4,128)S(1)} %gather_fusion.1), channel_id=1, source_target_pairs={{16,0},{32,16},{48,32},{64,48},{80,64},{96,80},{112,96},{128,112},... | collective-permute-start | bytes 331784 | tf_op jit(solution)/shard_map/ppermute | solution.py:21
  5.9 65.0 %collective-permute-start = (f32[4,3,2304]{2,0,1:T(4,128)S(1)}, f32[4,3,2304]{2,0,1:T(4,128)S(1)}, u32[]{:S(2)}, u32[]{:S(2)}) collective-permute-start(f32[4,3,2304]{2,0,1:T(4,128)S(1)} %gather_fusion), channel_id=1, source_target_pairs={{0,16},{16,32},{32,48},{48,64},{64,80},{80,96},{96,112},{112,128},... | collective-permute-start | bytes 331784 | tf_op jit(solution)/shard_map/ppermute | solution.py:21
  8.5 1.1 copy-start.31
  8.8 0.7 copy-start.30
  8.8 1.4 copy-start.27
  10.4 59.6 %copy-start.13 = (f32[2304]{0:T(1024)}, f32[2304]{0:T(1024)S(1)}, u32[]{:S(2)}) copy-start(f32[2304]{0:T(1024)S(1)} %mul.1491) | copy-start | bytes 27652
  10.6 2.4 copy-start.15
  10.7 2.3 copy-start.16
  10.7 2.3 copy-start.18
  10.7 2.3 copy-start.20
  10.7 2.3 copy-start.21
  10.8 2.3 copy-start.22
  10.8 2.3 copy-start.23
  11.0 2.1 copy-start.1
  11.0 2.1 copy-start.2
  11.0 2.1 copy-start.3
  11.0 2.1 copy-start.4
  11.0 2.1 copy-start.5
  11.0 2.1 copy-start.6
  11.0 2.1 copy-start.7
  11.0 2.1 copy-start.8
  11.0 2.1 copy-start.9
  11.1 2.1 copy-start.10
  11.1 2.1 copy-start.11
  11.1 2.1 copy-start.12
  70.4 0.8 copy-start.26
  87.1 47.9 %copy-start.14 = (f32[2304]{0:T(1024)S(1)}, f32[2304]{0:T(1024)}, u32[]{:S(2)}) copy-start(f32[2304]{0:T(1024)} %copy-done.13) | copy-start | bytes 27652
  135.1 9.0 %collective-permute-start.2 = (f32[16,1,2304]{2,1,0:T(1,128)S(1)}, f32[16,1,2304]{2,1,0:T(1,128)S(1)}, u32[]{:S(2)}, u32[]{:S(2)}) collective-permute-start(f32[16,1,2304]{2,1,0:T(1,128)S(1)} %get-tuple-element.81), channel_id=1, source_target_pairs={{1,0},{2,1},{3,2},{4,3},{5,4},{6,5},{7,6},{8,7},{9,8},{10,9},{11,1... | collective-permute-start | bytes 442376 | tf_op jit(solution)/shard_map/ppermute | solution.py:34
  138.3 17.8 %collective-permute-start.3 = (f32[16,1,2304]{2,1,0:T(1,128)S(1)}, f32[16,1,2304]{2,1,0:T(1,128)S(1)}, u32[]{:S(2)}, u32[]{:S(2)}) collective-permute-start(f32[16,1,2304]{2,1,0:T(1,128)S(1)} %get-tuple-element.82), channel_id=1, source_target_pairs={{0,1},{1,2},{2,3},{3,4},{4,5},{5,6},{6,7},{7,8},{8,9},{9,10},{10,1... | collective-permute-start | bytes 442376 | tf_op jit(solution)/shard_map/ppermute | solution.py:32
  215.4 7.2 %collective-permute-start.4 = (f32[16,1,2304]{2,1,0:T(1,128)S(1)}, f32[16,1,2304]{2,1,0:T(1,128)S(1)}, u32[]{:S(2)}, u32[]{:S(2)}) collective-permute-start(f32[16,1,2304]{2,1,0:T(1,128)S(1)} %get-tuple-element.61), channel_id=1, source_target_pairs={{1,0},{2,1},{3,2},{4,3},{5,4},{6,5},{7,6},{8,7},{9,8},{10,9},{11,1... | collective-permute-start | bytes 442376 | tf_op jit(solution)/shard_map/ppermute | solution.py:34
  218.5 15.0 %collective-permute-start.5 = (f32[16,1,2304]{2,1,0:T(1,128)S(1)}, f32[16,1,2304]{2,1,0:T(1,128)S(1)}, u32[]{:S(2)}, u32[]{:S(2)}) collective-permute-start(f32[16,1,2304]{2,1,0:T(1,128)S(1)} %get-tuple-element.62), channel_id=1, source_target_pairs={{0,1},{1,2},{2,3},{3,4},{4,5},{5,6},{6,7},{7,8},{8,9},{9,10},{10,1... | collective-permute-start | bytes 442376 | tf_op jit(solution)/shard_map/ppermute | solution.py:32
  (19 other events, 12.9 us)
where the time goes:
time: 245 us; the launch traced here: 244 us
  blocking collectives  148 us (60%)
  other arithmetic  31.8 us (13%)
  waiting for transfers between devices  24.1 us (10%)
  local copies, waits for them, and re-layouts  21 us (9%)
  starting transfers between devices  16.4 us (7%)
    psum x2, blocking collectives, body(): moments_sum = lax.psum(moment_sums(moved, weights), 'vel')  95.6 us
    psum x1, blocking collectives, body(): totals = lax.psum((jnp.stack(out_list), jnp.stack(in_list)), 'vel')  52.9 us
    ppermute x2, waiting for transfers between devices, padded_2(): lax.ppermute(tail, axis, [(i, (i + 1) % count) for i in range(ends)])  23 us
    add x2, other arithmetic, fp_update(): centre + per_cell(collision_frequency) * (drift + diffusion / (GRID_STEP...  9.38 us
    gather x6, local copies, waits for them, and re-layouts, body(): extended[neighbours[face_slot]]  8.12 us
    ppermute x2, starting transfers between devices, padded_2(): lax.ppermute(head, axis, [((i + 1) % count, i) for i in range(ends)])  6.28 us
    sub x1, other arithmetic, body(): moved = distribution - TIME_STEP * flux_sum / per_cell(cell_volume)  5.85 us
    ppermute x2, starting transfers between devices, padded_2(): lax.ppermute(tail, axis, [(i, (i + 1) % count) for i in range(ends)])  5.81 us
  transfers between devices with their start and end apart: 6, of which 3 were waited for; matrix products, arithmetic and copies ran while one was open for 5% of the time, Pallas kernels for 0%

commit v1 on v0

v1 whole, which is shorter than its diff:
```python
import functools

import jax
import jax.numpy as jnp
from jax import lax
from jax.experimental import pallas as pl
from jax.experimental.pallas import tpu as pltpu
from jax.sharding import PartitionSpec as P

NV = 48
FLAT = NV * NV
STEP = 0.25
DT = 0.02
RATE = 0.002
FACES = 6
HALO = 4
CELLS = 16
PLANES = 3
MARGIN = 128
WIDE = FLAT + 2 * MARGIN
VELS = 16
MESH = pl.DeviceIdType.MESH
F32 = jnp.float32
BF16 = jnp.bfloat16


def split2(x):
    hi = x.astype(BF16)
    return hi, (x - hi.astype(F32)).astype(BF16)


def split3(x):
    hi = x.astype(BF16)
    r = x - hi.astype(F32)
    mid = r.astype(BF16)
    return hi, mid, (r - mid.astype(F32)).astype(BF16)


def lane_sums(acc):
    ones = jnp.ones((16, 128), BF16)
    total = None
    for part in split3(acc):
        term = lax.dot_general(ones, part, (((1,), (1,)), ((), ())), preferred_element_type=F32)
        total = term if total is None else total + term
    return total[0:1]


def spread(row, sel):
    k = row.shape[1]
    lane = lax.broadcasted_iota(jnp.int32, (CELLS, k), 1)
    cell = lax.broadcasted_iota(jnp.int32, (CELLS, k), 0)
    own = jnp.where((lane & (CELLS - 1)) == cell, jnp.broadcast_to(row, (CELLS, k)), 0.0)
    stacked = jnp.concatenate(split3(own), axis=0)
    out = jnp.dot(stacked, sel, preferred_element_type=F32)
    return out[0:16] + out[16:32] + out[32:48]


def rep(x, n):
    return jnp.concatenate([x] * n, axis=1)


def kernel(
    dist, free, area, vol, nb, wall, send, out,
    distv, hs, hr, fa, fb, fc, yt, zt, mt, prm, sb, lhs, sel, fsend, frecv, msend, mrecv,
    in_sem, out_sem, h_ssem, h_rsem, f_ssem, f_rsem, m_ssem, m_rsem, p_ssem, p_rsem,
):
    space = lax.axis_index("space")
    vel = lax.axis_index("vel")
    blocks = lax.axis_size("space")
    has_below, has_above = space > 0, space < blocks - 1
    has_left, has_right = vel > 0, vel < VELS - 1

    loads = [pltpu.make_async_copy(dist.at[p], distv.at[p], in_sem.at[p]) for p in range(PLANES)]
    for copy in loads:
        copy.start()

    barrier = pltpu.get_barrier_semaphore()
    for d in range(1, VELS):
        pl.semaphore_signal(barrier, 1, device_id=(space, lax.rem(vel + d, VELS)), device_id_type=MESH)

    @pl.when(has_below)
    def _():
        pl.semaphore_signal(barrier, 1, device_id=(space - 1, vel), device_id_type=MESH)

    @pl.when(has_above)
    def _():
        pl.semaphore_signal(barrier, 1, device_id=(space + 1, vel), device_id_type=MESH)

    flat = lax.broadcasted_iota(jnp.int32, (CELLS, FLAT), 1).astype(F32)
    row = jnp.floor((flat + 0.5) / NV)
    y = (row - (NV - 1) / 2.0) * STEP
    z = (flat - row * NV - (NV - 1) / 2.0) * STEP
    yt[...] = y
    zt[...] = z
    mt[...] = jnp.exp(-(y * y + z * z) / 2.0)
    krow = lax.broadcasted_iota(jnp.int32, (256, 1280), 0)
    kcol = lax.broadcasted_iota(jnp.int32, (256, 1280), 1)
    sel[...] = jnp.where((krow >> 4) == (kcol >> 7), 1.0, 0.0).astype(BF16)
    for buf in (fa, fb):
        for plane in range(PLANES + 2):
            buf[plane, :, 0:MARGIN] = jnp.zeros((CELLS, MARGIN), F32)
            buf[plane, :, MARGIN + FLAT :] = jnp.zeros((CELLS, MARGIN), F32)

    @pl.when(jnp.logical_not(has_left))
    def _():
        fa[0] = jnp.zeros((CELLS, WIDE), F32)
        fb[0] = jnp.zeros((CELLS, WIDE), F32)

    @pl.when(jnp.logical_not(has_right))
    def _():
        fa[PLANES + 1] = jnp.zeros((CELLS, WIDE), F32)
        fb[PLANES + 1] = jnp.zeros((CELLS, WIDE), F32)

    prm[...] = jnp.zeros((32, 128), F32)
    for i in range(3):
        prm[6 * i : 6 * i + 6, 0:CELLS] = area[i]
    prm[18:24, 0:CELLS] = nb[...].astype(F32)
    prm[24:30, 0:CELLS] = wall[...].astype(F32)
    prm[30:31, 0:CELLS] = DT / vol[...]
    cols = prm[...].T[0:CELLS]
    for r in range(31):
        sb[r] = jnp.broadcast_to(cols[:, r : r + 1], (CELLS, 128))

    for copy in loads:
        copy.wait()
    for p in range(PLANES):
        for side in range(2):
            for r in range(HALO):
                hs[side, p, r : r + 1, :] = distv[p, pl.ds(send[side, r], 1), :]

    peers = VELS - 1 + has_below.astype(jnp.int32) + has_above.astype(jnp.int32)
    pl.semaphore_wait(barrier, peers)

    def halo(side, target):
        return pltpu.make_async_remote_copy(
            src_ref=hs.at[side], dst_ref=hr.at[1 - side], send_sem=h_ssem.at[side], recv_sem=h_rsem.at[1 - side],
            device_id=(target, vel), device_id_type=MESH,
        )

    @pl.when(has_above)
    def _():
        halo(1, space + 1).start()

    @pl.when(has_below)
    def _():
        halo(0, space - 1).start()

    @pl.when(jnp.logical_not(has_below))
    def _():
        for p in range(PLANES):
            hr[0, p] = jnp.broadcast_to(free[p : p + 1, :], (HALO, FLAT))

    @pl.when(jnp.logical_not(has_above))
    def _():
        for p in range(PLANES):
            hr[1, p] = jnp.broadcast_to(free[p : p + 1, :], (HALO, FLAT))

    xs = [((vel * PLANES + p).astype(F32) - (NV - 1) / 2.0) * STEP for p in range(PLANES)]
    mx = [jnp.exp(jnp.full((CELLS, 128), -0.5, F32) * (x * x)) for x in xs]

    def gather_copy(src, dst, ssem, rsem, d):
        return pltpu.make_async_remote_copy(
            src_ref=src, dst_ref=dst.at[d], send_sem=ssem.at[d], recv_sem=rsem.at[d],
            device_id=(space, lax.rem(vel + d, VELS)), device_id_type=MESH,
        )

    def total(src, dst, ssem, rsem):
        acc = src[...]
        for d in range(1, VELS):
            gather_copy(src, dst, ssem, rsem, d).wait_recv()
            acc = acc + dst[d]
        return acc

    def flux_plane(p, carry):
        sx = [sb[s] * xs[p] for s in range(FACES)]

        def step(t, carry):
            off = pl.multiple_of(t * 256, 128)
            outs, ins = list(carry[:FACES]), list(carry[FACES:])
            for j in range(2):
                o = pl.ds(off + 128 * j, 128)
                dd, yy, zz = distv[p, :, o], yt[:, o], zt[:, o]
                mm = mt[:, o] * mx[p]
                for s in range(FACES):
                    w = jnp.maximum(sx[s] + sb[6 + s] * yy + sb[12 + s] * zz, 0.0)
                    outs[s] = outs[s] + w * dd
                    ins[s] = ins[s] + w * mm
            return tuple(outs + ins)

        return lax.fori_loop(0, FLAT // 256, step, carry)

    carry = tuple(jnp.zeros((CELLS, 128), F32) for _ in range(2 * FACES))
    for p in range(PLANES):
        carry = flux_plane(p, carry)
    fsend[0:1, 0:96] = lane_sums(jnp.concatenate(carry[:FACES], axis=0))
    fsend[0:1, 128:224] = lane_sums(jnp.concatenate(carry[FACES:], axis=0))
    fsend[0:1, 96:128] = jnp.zeros((1, 32), F32)
    fsend[0:1, 224:256] = jnp.ones((1, 32), F32)
    for d in range(1, VELS):
        gather_copy(fsend, frecv, f_ssem, f_rsem, d).start()
    flux = total(fsend, frecv, f_ssem, f_rsem)
    ratio = spread(flux[:, 0:128] / jnp.where(flux[:, 128:256] > 0.0, flux[:, 128:256], 1.0), sel[0:128, 0:768])

    lane = lax.broadcasted_iota(jnp.int32, (CELLS, 64), 1) & 31
    for s in range(FACES):
        r = ratio[:, 128 * s : 128 * s + 64]
        r_hi = r.astype(BF16).astype(F32)
        at_wall = jnp.where(lane == 24, r_hi, jnp.where(lane == 25, r - r_hi, 0.0))
        inside = jnp.where(lane.astype(F32) == sb[18 + s][:, 0:64], 1.0, 0.0)
        lhs[16 * s : 16 * s + 16, :] = jnp.where(sb[24 + s][:, 0:64] > 0.5, at_wall, inside).astype(BF16)

    @pl.when(has_below)
    def _():
        halo(1, space + 1).wait_recv()

    @pl.when(has_above)
    def _():
        halo(0, space - 1).wait_recv()

    zero6 = tuple(jnp.zeros((CELLS, 128), F32) for _ in range(6))

    def add_moments(acc, f, yy, zz):
        fy, fz = f * yy, f * zz
        return (acc[0] + f, acc[1] + fy, acc[2] + fz, acc[3] + fy * yy, acc[4] + fz * zz, acc[5] + fy * zz)

    def send_moments(k, sums):
        m0 = sums[0][0] + sums[1][0] + sums[2][0]
        wx = [sums[p][0] * xs[p] for p in range(PLANES)]
        m1 = wx[0] + wx[1] + wx[2]
        m4 = wx[0] * xs[0] + wx[1] * xs[1] + wx[2] * xs[2]

        def plain(i):
            return sums[0][i] + sums[1][i] + sums[2][i]

        def timesx(i):
            return sums[0][i] * xs[0] + sums[1][i] * xs[1] + sums[2][i] * xs[2]

        acc = [m0, m1, plain(1), plain(2), m4, plain(3), plain(4), timesx(1), timesx(2), plain(5)]
        msend[k, 0:1, 0:160] = lane_sums(jnp.concatenate(acc, axis=0))
        msend[k, 0:1, 160:256] = jnp.zeros((1, 96), F32)
        for d in range(1, VELS):
            gather_copy(msend.at[k], mrecv.at[k], m_ssem.at[k], m_rsem.at[k], d).start()

    def plane_copy(k, buf, right):
        src, dst = (PLANES, 0) if right else (1, PLANES + 1)
        lanes = pl.ds(MARGIN, FLAT)
        i = 1 if right else 0
        return pltpu.make_async_remote_copy(
            src_ref=buf.at[src, :, lanes], dst_ref=buf.at[dst, :, lanes],
            send_sem=p_ssem.at[k, i], recv_sem=p_rsem.at[k, i],
            device_id=(space, vel + 1 if right else vel - 1), device_id_type=MESH,
        )

    def send_plane(k, buf, right):
        @pl.when(has_right if right else has_left)
        def _():
            plane_copy(k, buf, right).start()

    def recv_planes(k, buf):
        @pl.when(has_left)
        def _():
            plane_copy(k, buf, True).wait_recv()

        @pl.when(has_right)
        def _():
            plane_copy(k, buf, False).wait_recv()

    def moved_plane(p):
        sx = [sb[s] * xs[p] for s in range(FACES)]
        scale = sb[30]

        def step(t, acc):
            off = pl.multiple_of(t * 256, 128)
            o = pl.ds(off, 256)
            mm = mt[0:8, o] * rep(mx[p][0:8], 2)
            ext = jnp.concatenate([distv[p, :, o], hr[0, p, :, o], hr[1, p, :, o], mm], axis=0)
            picked = jnp.dot(lhs[...], jnp.concatenate(split2(ext), axis=0), preferred_element_type=F32)
            for j in range(2):
                o = pl.ds(off + 128 * j, 128)
                dd, yy, zz = distv[p, :, o], yt[:, o], zt[:, o]
                out_sum, in_sum = None, None
                for s in range(FACES):
                    w = sx[s] + sb[6 + s] * yy + sb[12 + s] * zz
                    up = jnp.maximum(w, 0.0)
                    term = (w - up) * picked[16 * s : 16 * s + 16, 128 * j : 128 * j + 128]
                    out_sum = up if s == 0 else out_sum + up
                    in_sum = term if s == 0 else in_sum + term
                f = dd - scale * (out_sum * dd + in_sum)
                fa[p + 1, :, pl.ds(off + 128 * j + MARGIN, 128)] = f
                acc = add_moments(acc, f, yy, zz)
            return acc

        return lax.fori_loop(0, FLAT // 256, step, zero6)

    sums = [None] * PLANES
    sums[0] = moved_plane(0)
    send_plane(0, fa, False)
    sums[2] = moved_plane(2)
    send_plane(0, fa, True)
    sums[1] = moved_plane(1)
    send_moments(0, sums)

    def coefficients(k):
        row = total(msend.at[k], mrecv.at[k], m_ssem.at[k], m_rsem.at[k])
        allm = spread(row, sel[...])
        m = [allm[:, 128 * i : 128 * i + 128] for i in range(10)]
        inv = 1.0 / m[0]
        ux, uy, uz = m[1] * inv, m[2] * inv, m[3] * inv
        cxx, cyy, czz = m[4] * inv - ux * ux, m[5] * inv - uy * uy, m[6] * inv - uz * uz
        cxy, cxz, cyz = m[7] * inv - ux * uy, m[8] * inv - ux * uz, m[9] * inv - uy * uz
        theta = (cxx + cyy + czz) / 3.0
        a = (RATE * STEP**3) * m[0] * jnp.exp(0.19 * jnp.log(theta))
        lx, ly, lz = 0.5 * (theta + cxx), 0.5 * (theta + cyy), 0.5 * (theta + czz)
        return dict(
            ux=ux, a=a, k0=1.0 - 32.0 * a * (lx + ly + lz), lx=16.0 * a * lx,
            ys=a * (16.0 * ly + 0.5), a2=2.0 * a, a2uy=2.0 * a * uy, a2uz=2.0 * a * uz, zq=16.0 * a * lz,
            gxy=4.0 * a * cxy, gxz=4.0 * a * cxz, gyz=4.0 * a * cyz,
        )

    width = 384

    def relax_plane(src, dst, dst_off, p, c, moments):
        n = width // 128
        drift_n = c["a2"] * (xs[p] + STEP - c["ux"]) + c["lx"]
        drift_p = c["lx"] - c["a2"] * (xs[p] - STEP - c["ux"])
        kn, kp, k0 = rep(drift_n, n), rep(drift_p, n), rep(c["k0"], n)
        ys, a2, a2uy, a2uz, zq = (rep(c[q], n) for q in ("ys", "a2", "a2uy", "a2uz", "zq"))
        gxy, gxz, gyz = (rep(c[q], n) for q in ("gxy", "gxz", "gyz"))
        lanes = lax.broadcasted_iota(jnp.int32, (CELLS, width), 1)

        def step(t, acc):
            off = pl.multiple_of(t * width, 128)
            win = pl.ds(off, width + 2 * MARGIN)
            cen = pl.ds(off, width)
            cw, nw, pw = src[p + 1, :, win], src[p + 2, :, win], src[p, :, win]
            xw = nw - pw
            yy, zz = yt[:, cen], zt[:, cen]
            total_w = width + 2 * MARGIN

            def up(v):
                return pltpu.roll(v, total_w - NV, 1)[:, MARGIN : MARGIN + width]

            def down(v):
                return pltpu.roll(v, NV, 1)[:, MARGIN : MARGIN + width]

            cc, nn, pp = (v[:, MARGIN : MARGIN + width] for v in (cw, nw, pw))
            u, d = up(cw), down(cw)
            diff = u - d
            res = k0 * cc + kn * nn + kp * pp
            res = res + ys * (u + d) + (a2 * yy - a2uy) * diff + gxy * (up(xw) - down(xw))
            cross = gxz * (nn - pp) + gyz * diff
            zr = a2 * zz - a2uz
            plus = (zq + zr) * cc + cross
            minus = (zq - zr) * cc - cross
            edge = (NV - 1) / 2.0 * STEP
            res = res + jnp.where(zz < edge - 0.1, pltpu.roll(plus, width - 1, 1), 0.0)
            res = res + jnp.where(zz > 0.1 - edge, pltpu.roll(minus, 1, 1), 0.0)
            dst[dst_off + p, :, pl.ds(off + (MARGIN if dst_off else 0), width)] = res
            if moments:
                for j in range(n):
                    q = slice(128 * j, 128 * j + 128)
                    acc = add_moments(acc, res[:, q], yy[:, q], zz[:, q])
            return acc

        del lanes
        return lax.fori_loop(0, FLAT // width, step, zero6 if moments else 0)

    c = coefficients(0)
    recv_planes(0, fa)
    sums[0] = relax_plane(fa, fb, 1, 0, c, True)
    send_plane(1, fb, False)
    sums[2] = relax_plane(fa, fb, 1, 2, c, True)
    send_plane(1, fb, True)
    sums[1] = relax_plane(fa, fb, 1, 1, c, True)
    send_moments(1, sums)
    c = coefficients(1)
    relax_plane(fb, fc, 0, 1, c, False)
    recv_planes(1, fb)
    stores = [pltpu.make_async_copy(fc.at[p], out.at[p], out_sem.at[p]) for p in range(PLANES)]
    stores[1].start()
    for p in (0, 2):
        relax_plane(fb, fc, 0, p, c, False)
        stores[p].start()

    @pl.when(has_above)
    def _():
        halo(1, space + 1).wait_send()

    @pl.when(has_below)
    def _():
        halo(0, space - 1).wait_send()

    for d in range(1, VELS):
        gather_copy(fsend, frecv, f_ssem, f_rsem, d).wait_send()
        for k in range(2):
            gather_copy(msend.at[k], mrecv.at[k], m_ssem.at[k], m_rsem.at[k], d).wait_send()
    for k, buf in ((0, fa), (1, fb)):
        for right in (False, True):

            @pl.when(has_right if right else has_left)
            def _():
                plane_copy(k, buf, right).wait_send()

    for copy in stores:
        copy.wait()


def body(distribution, freestream, face_area, cell_volume, neighbours, wall_flags, send_cells):
    dma = pltpu.SemaphoreType.DMA
    vmem = pl.BlockSpec(memory_space=pltpu.VMEM)
    anyw = pl.BlockSpec(memory_space=pl.ANY)
    new = pl.pallas_call(
        kernel,
        out_shape=jax.ShapeDtypeStruct((PLANES, CELLS, FLAT), F32),
        in_specs=[anyw, vmem, vmem, vmem, vmem, vmem, pl.BlockSpec(memory_space=pltpu.SMEM)],
        out_specs=anyw,
        scratch_shapes=[
            pltpu.VMEM((PLANES, CELLS, FLAT), F32),
            pltpu.VMEM((2, PLANES, HALO, FLAT), F32),
            pltpu.VMEM((2, PLANES, HALO, FLAT), F32),
            pltpu.VMEM((PLANES + 2, CELLS, WIDE), F32),
            pltpu.VMEM((PLANES + 2, CELLS, WIDE), F32),
            pltpu.VMEM((PLANES, CELLS, FLAT), F32),
            pltpu.VMEM((CELLS, FLAT), F32),
            pltpu.VMEM((CELLS, FLAT), F32),
            pltpu.VMEM((CELLS, FLAT), F32),
            pltpu.VMEM((32, 128), F32),
            pltpu.VMEM((32, CELLS, 128), F32),
            pltpu.VMEM((96, 64), BF16),
            pltpu.VMEM((256, 1280), BF16),
            pltpu.VMEM((1, 256), F32),
            pltpu.VMEM((VELS, 1, 256), F32),
            pltpu.VMEM((2, 1, 256), F32),
            pltpu.VMEM((2, VELS, 1, 256), F32),
            dma((PLANES,)), dma((PLANES,)), dma((2,)), dma((2,)),
            dma((VELS,)), dma((VELS,)), dma((2, VELS)), dma((2, VELS)), dma((2, 2)), dma((2, 2)),
        ],
        compiler_params=pltpu.CompilerParams(
            collective_id=0, has_side_effects=True, vmem_limit_bytes=24 * 1024 * 1024
        ),
    )(
        jnp.transpose(distribution, (1, 0, 2)), freestream, face_area, cell_volume.reshape(1, CELLS), neighbours,
        wall_flags, send_cells,
    )
    return jnp.transpose(new, (1, 0, 2))


def solution(mesh):
    in_specs = (
        P("space", "vel", None),
        P("vel", None),
        P(None, None, "space"),
        P("space"),
        P(None, "space"),
        P(None, "space"),
        P(None, "space"),
    )
    out_specs = P("space", "vel", None)
    return jax.shard_map(body, mesh=mesh, in_specs=in_specs, out_specs=out_specs, check_vma=False)
```

time: 245 us -> 73.1 us (0.30)
  the two profiles are of different devices: /device:TPU:422 before, /device:TPU:1 now
where the time goes in v1:
time: 73.1 us; the launch traced here: 72.4 us
  Pallas kernels  67.1 us (92%)
  local copies, waits for them, and re-layouts  5.3 us (7%)
    pallas_call x1, Pallas kernels, body(): pl.pallas_call(kernel, out_shape=jax.ShapeDtypeStruct((PLANES, CELLS, FLA...  67.1 us
    unnamed x15, local copies, waits for them, and re-layouts  5.3 us

profile of v1, /device:TPU:1, one launch (start us, length us, event | category | flops | bytes accessed | tf_op | source)
XLA Modules:
  0.0 72.4 jit_solution(7834140410783545455)
XLA Ops:
  0.0 0.0 copy-start.5
  0.0 0.0 copy-start.6
  0.0 0.7 copy-done.5
  0.7 0.0 copy-done.6
  0.7 0.0 copy-start
  0.7 1.0 %copy-done = f32[16,3,2304]{2,0,1:T(8,128)S(1)} copy-done((f32[16,3,2304]{2,0,1:T(8,128)S(1)}, f32[16,3,2304]{2,0,1:T(8,128)}, u32[]{:S(2)}) %copy-start) | copy-done | bytes 442392
  1.7 0.0 copy-start.1
  1.7 0.8 %copy-done.1 = f32[3,2304]{1,0:T(4,128)S(1)} copy-done((f32[3,2304]{1,0:T(4,128)S(1)}, f32[3,2304]{1,0:T(4,128)}, u32[]{:S(2)}) %copy-start.1) | copy-done | bytes 27672
  2.5 0.0 copy-start.2
  2.5 0.7 copy-done.2
  3.2 0.0 copy-start.3
  3.2 0.7 copy-done.3
  3.9 0.0 copy-start.4
  3.9 0.7 copy-done.4
  4.5 67.1 %shard_map.73 = f32[3,16,2304]{2,1,0:T(8,128)S(1)} custom-call(f32[3,16,2304]{2,1,0:T(8,128)S(1)} %bitcast.4, f32[3,2304]{1,0:T(4,128)S(1)} %copy-done.1, f32[3,6,16]{2,1,0:T(8,128)S(1)} %copy-done.2, f32[1,16]{1,0:T(1,128)S(1)} %bitcast.5, s32[6,16]{1,0:T(8,128)S(1)} %copy-done.3, s32[6,16]{1,0:T(8,128)S(1)} %copy-done.4, s32[2,4]{1,0:T(2,128)S(1)} %copy-done.5), custom_call_target="tpu_custom_call" | custom-call | tf_op jit(solution)/shard_map/pallas_call | solution.py:412
  71.6 0.8 %copy.9 = f32[16,3,2304]{2,0,1:T(8,128)} copy(f32[16,3,2304]{2,0,1:T(8,128)S(1)} %bitcast.3) | data formatting | bytes 884736
Async XLA Ops:
  0.0 0.7 copy-start.5
  0.0 0.7 copy-start.6
  0.7 1.0 %copy-start = (f32[16,3,2304]{2,0,1:T(8,128)S(1)}, f32[16,3,2304]{2,0,1:T(8,128)}, u32[]{:S(2)}) copy-start(f32[16,3,2304]{2,0,1:T(8,128)} %param.7) | copy-start | bytes 1327108
  1.7 0.8 %copy-start.1 = (f32[3,2304]{1,0:T(4,128)S(1)}, f32[3,2304]{1,0:T(4,128)}, u32[]{:S(2)}) copy-start(f32[3,2304]{1,0:T(4,128)} %free.1) | copy-start | bytes 82948
  2.5 0.7 copy-start.2
  3.2 0.7 copy-start.3
  3.9 0.7 copy-start.4

commit v2 on v1

--- a/solution.py
+++ b/solution.py
@@ -19,6 +19,8 @@
 MARGIN = 128
 WIDE = FLAT + 2 * MARGIN
 VELS = 16
+LANES = 4
+PARTS = ((9, 13), (13, 16), (16, 18), (0, 9))
 MESH = pl.DeviceIdType.MESH
 F32 = jnp.float32
 BF16 = jnp.bfloat16
@@ -60,9 +62,10 @@
 
 
 def kernel(
-    dist, free, area, vol, nb, wall, send, out,
-    distv, hs, hr, fa, fb, fc, yt, zt, mt, prm, sb, lhs, sel, fsend, frecv, msend, mrecv,
+    dist, free_h, area_h, vol_h, nb_h, wall_h, send_h, out,
+    free, area, vol, nb, wall, send, distv, hs, hr, fa, fb, fc, relay, yt, zt, mt, prm, sb, lhs, sel, fsend, frecv, msend, mrecv,
     in_sem, out_sem, h_ssem, h_rsem, f_ssem, f_rsem, m_ssem, m_rsem, p_ssem, p_rsem,
+    s_sem, z_ssem, z_rsem, r_ssem, r_rsem,
 ):
     space = lax.axis_index("space")
     vel = lax.axis_index("vel")
@@ -71,7 +74,13 @@
     has_left, has_right = vel > 0, vel < VELS - 1
 
     loads = [pltpu.make_async_copy(dist.at[p], distv.at[p], in_sem.at[p]) for p in range(PLANES)]
-    for copy in loads:
+    small = [
+        pltpu.make_async_copy(src, dst, s_sem.at[i])
+        for i, (src, dst) in enumerate(
+            ((area_h, area), (nb_h, nb), (wall_h, wall), (vol_h, vol), (send_h, send), (free_h, free))
+        )
+    ]
+    for copy in small + loads:
         copy.start()
 
     barrier = pltpu.get_barrier_semaphore()
@@ -111,6 +120,9 @@
         fa[PLANES + 1] = jnp.zeros((CELLS, WIDE), F32)
         fb[PLANES + 1] = jnp.zeros((CELLS, WIDE), F32)
 
+    for copy in small:
+        copy.wait()
+
     prm[...] = jnp.zeros((32, 128), F32)
     for i in range(3):
         prm[6 * i : 6 * i + 6, 0:CELLS] = area[i]
@@ -127,33 +139,6 @@
         for side in range(2):
             for r in range(HALO):
                 hs[side, p, r : r + 1, :] = distv[p, pl.ds(send[side, r], 1), :]
-
-    peers = VELS - 1 + has_below.astype(jnp.int32) + has_above.astype(jnp.int32)
-    pl.semaphore_wait(barrier, peers)
-
-    def halo(side, target):
-        return pltpu.make_async_remote_copy(
-            src_ref=hs.at[side], dst_ref=hr.at[1 - side], send_sem=h_ssem.at[side], recv_sem=h_rsem.at[1 - side],
-            device_id=(target, vel), device_id_type=MESH,
-        )
-
-    @pl.when(has_above)
-    def _():
-        halo(1, space + 1).start()
-
-    @pl.when(has_below)
-    def _():
-        halo(0, space - 1).start()
-
-    @pl.when(jnp.logical_not(has_below))
-    def _():
-        for p in range(PLANES):
-            hr[0, p] = jnp.broadcast_to(free[p : p + 1, :], (HALO, FLAT))
-
-    @pl.when(jnp.logical_not(has_above))
-    def _():
-        for p in range(PLANES):
-            hr[1, p] = jnp.broadcast_to(free[p : p + 1, :], (HALO, FLAT))
 
     xs = [((vel * PLANES + p).astype(F32) - (NV - 1) / 2.0) * STEP for p in range(PLANES)]
     mx = [jnp.exp(jnp.full((CELLS, 128), -0.5, F32) * (x * x)) for x in xs]
@@ -196,6 +181,33 @@
     fsend[0:1, 128:224] = lane_sums(jnp.concatenate(carry[FACES:], axis=0))
     fsend[0:1, 96:128] = jnp.zeros((1, 32), F32)
     fsend[0:1, 224:256] = jnp.ones((1, 32), F32)
+    peers = VELS - 1 + has_below.astype(jnp.int32) + has_above.astype(jnp.int32)
+    pl.semaphore_wait(barrier, peers)
+
+    def halo(side, target):
+        return pltpu.make_async_remote_copy(
+            src_ref=hs.at[side], dst_ref=hr.at[1 - side], send_sem=h_ssem.at[side], recv_sem=h_rsem.at[1 - side],
+            device_id=(target, vel), device_id_type=MESH,
+        )
+
+    @pl.when(has_above)
+    def _():
+        halo(1, space + 1).start()
+
+    @pl.when(has_below)
+    def _():
+        halo(0, space - 1).start()
+
+    @pl.when(jnp.logical_not(has_below))
+    def _():
+        for p in range(PLANES):
+            hr[0, p] = jnp.broadcast_to(free[p : p + 1, :], (HALO, FLAT))
+
+    @pl.when(jnp.logical_not(has_above))
+    def _():
+        for p in range(PLANES):
+            hr[1, p] = jnp.broadcast_to(free[p : p + 1, :], (HALO, FLAT))
+
     for d in range(1, VELS):
         gather_copy(fsend, frecv, f_ssem, f_rsem, d).start()
     flux = total(fsend, frecv, f_ssem, f_rsem)
@@ -241,8 +253,20 @@
         for d in range(1, VELS):
             gather_copy(msend.at[k], mrecv.at[k], m_ssem.at[k], m_rsem.at[k], d).start()
 
-    def plane_copy(k, buf, right):
-        src, dst = (PLANES, 0) if right else (1, PLANES + 1)
+    y_at, z_at = lax.rem(vel, LANES), vel // LANES
+
+    def sides(right):
+        return (LANES - 1, 0, 1, z_at < LANES - 1) if right else (0, LANES - 1, -1, z_at > 0)
+
+    def ends(right):
+        return (PLANES, 0) if right else (1, PLANES + 1)
+
+    def lanes_of(right, q):
+        first, last = PARTS[q if right else LANES - 1 - q]
+        return first, last - first
+
+    def near_copy(k, buf, right):
+        src, dst = ends(right)
         lanes = pl.ds(MARGIN, FLAT)
         i = 1 if right else 0
         return pltpu.make_async_remote_copy(
@@ -251,19 +275,92 @@
             device_id=(space, vel + 1 if right else vel - 1), device_id_type=MESH,
         )
 
+    def part_copy(k, buf, right, q):
+        home, other, dz, _ = sides(right)
+        src, dst = ends(right)
+        first, count = lanes_of(right, q)
+        lanes = pl.ds(MARGIN + 128 * first, 128 * count)
+        i = 1 if right else 0
+        if q == home:
+            dst_ref, recv, to = buf.at[dst, :, lanes], z_rsem.at[k, i, q], (z_at + dz) * LANES + other
+        else:
+            dst_ref, recv, to = relay.at[k, i, :, pl.ds(0, 128 * count)], r_rsem.at[k, i], z_at * LANES + q
+        return pltpu.make_async_remote_copy(
+            src_ref=buf.at[src, :, lanes], dst_ref=dst_ref, send_sem=z_ssem.at[k, i, q], recv_sem=recv,
+            device_id=(space, to), device_id_type=MESH,
+        )
+
+    def relay_copy(k, buf, right, q):
+        home, other, dz, _ = sides(right)
+        src, dst = ends(right)
+        first, count = lanes_of(right, q)
+        lanes = pl.ds(MARGIN + 128 * first, 128 * count)
+        i = 1 if right else 0
+        return pltpu.make_async_remote_copy(
+            src_ref=relay.at[k, i, :, pl.ds(0, 128 * count)], dst_ref=buf.at[dst, :, lanes],
+            send_sem=r_ssem.at[k, i], recv_sem=z_rsem.at[k, i, q],
+            device_id=(space, (z_at + dz) * LANES + other), device_id_type=MESH,
+        )
+
     def send_plane(k, buf, right):
-        @pl.when(has_right if right else has_left)
+        home, _, _, inner = sides(right)
+
+        @pl.when(y_at != home)
         def _():
-            plane_copy(k, buf, right).start()
+            near_copy(k, buf, right).start()
+
+        @pl.when((y_at == home) & inner)
+        def _():
+            for q in range(LANES):
+                part_copy(k, buf, right, q).start()
+
+    def pass_on(k, buf):
+        for right in (True, False):
+            home, _, _, inner = sides(right)
+            for q in range(LANES):
+                if q != home:
+
+                    @pl.when((y_at == q) & inner)
+                    def _():
+                        part_copy(k, buf, right, q).wait_recv()
+                        relay_copy(k, buf, right, q).start()
 
     def recv_planes(k, buf):
-        @pl.when(has_left)
-        def _():
-            plane_copy(k, buf, True).wait_recv()
-
-        @pl.when(has_right)
-        def _():
-            plane_copy(k, buf, False).wait_recv()
+        for right in (True, False):
+            home, other, _, _ = sides(right)
+            from_z = z_at > 0 if right else z_at < LANES - 1
+
+            @pl.when(y_at != other)
+            def _():
+                near_copy(k, buf, right).wait_recv()
+
+            @pl.when((y_at == other) & from_z)
+            def _():
+                for q in range(LANES):
+                    if q == home:
+                        part_copy(k, buf, right, q).wait_recv()
+                    else:
+                        relay_copy(k, buf, right, q).wait_recv()
+
+    def end_planes(k, buf):
+        for right in (True, False):
+            home, _, _, inner = sides(right)
+
+            @pl.when(y_at != home)
+            def _():
+                near_copy(k, buf, right).wait_send()
+
+            @pl.when((y_at == home) & inner)
+            def _():
+                for q in range(LANES):
+                    part_copy(k, buf, right, q).wait_send()
+
+            for q in range(LANES):
+                if q != home:
+
+                    @pl.when((y_at == q) & inner)
+                    def _():
+                        relay_copy(k, buf, right, q).wait_send()
 
     def moved_plane(p):
         sx = [sb[s] * xs[p] for s in range(FACES)]
@@ -290,7 +387,7 @@
                 acc = add_moments(acc, f, yy, zz)
             return acc
 
-        return lax.fori_loop(0, FLAT // 256, step, zero6)
+        return lax.fori_loop(0, FLAT // 256, step, zero6, unroll=True)
 
     sums = [None] * PLANES
     sums[0] = moved_plane(0)
@@ -299,6 +396,7 @@
     send_plane(0, fa, True)
     sums[1] = moved_plane(1)
     send_moments(0, sums)
+    pass_on(0, fa)
 
     def coefficients(k):
         row = total(msend.at[k], mrecv.at[k], m_ssem.at[k], m_rsem.at[k])
@@ -317,7 +415,7 @@
             gxy=4.0 * a * cxy, gxz=4.0 * a * cxz, gyz=4.0 * a * cyz,
         )
 
-    width = 384
+    width = 768
 
     def relax_plane(src, dst, dst_off, p, c, moments):
         n = width // 128
@@ -326,7 +424,6 @@
         kn, kp, k0 = rep(drift_n, n), rep(drift_p, n), rep(c["k0"], n)
         ys, a2, a2uy, a2uz, zq = (rep(c[q], n) for q in ("ys", "a2", "a2uy", "a2uz", "zq"))
         gxy, gxz, gyz = (rep(c[q], n) for q in ("gxy", "gxz", "gyz"))
-        lanes = lax.broadcasted_iota(jnp.int32, (CELLS, width), 1)
 
         def step(t, acc):
             off = pl.multiple_of(t * width, 128)
@@ -362,8 +459,7 @@
                     acc = add_moments(acc, res[:, q], yy[:, q], zz[:, q])
             return acc
 
-        del lanes
-        return lax.fori_loop(0, FLAT // width, step, zero6 if moments else 0)
+        return lax.fori_loop(0, FLAT // width, step, zero6 if moments else 0, unroll=True)
 
     c = coefficients(0)
     recv_planes(0, fa)
@@ -373,6 +469,7 @@
     send_plane(1, fb, True)
     sums[1] = relax_plane(fa, fb, 1, 1, c, True)
     send_moments(1, sums)
+    pass_on(1, fb)
     c = coefficients(1)
     relax_plane(fb, fc, 0, 1, c, False)
     recv_planes(1, fb)
@@ -394,33 +491,35 @@
         gather_copy(fsend, frecv, f_ssem, f_rsem, d).wait_send()
         for k in range(2):
             gather_copy(msend.at[k], mrecv.at[k], m_ssem.at[k], m_rsem.at[k], d).wait_send()
-    for k, buf in ((0, fa), (1, fb)):
-        for right in (False, True):
-
-            @pl.when(has_right if right else has_left)
-            def _():
-                plane_copy(k, buf, right).wait_send()
-
+    end_planes(0, fa)
+    end_planes(1, fb)
     for copy in stores:
         copy.wait()
 
 
 def body(distribution, freestream, face_area, cell_volume, neighbours, wall_flags, send_cells):
     dma = pltpu.SemaphoreType.DMA
-    vmem = pl.BlockSpec(memory_space=pltpu.VMEM)
+    hbm = pl.BlockSpec(memory_space=pltpu.HBM)
     anyw = pl.BlockSpec(memory_space=pl.ANY)
     new = pl.pallas_call(
         kernel,
         out_shape=jax.ShapeDtypeStruct((PLANES, CELLS, FLAT), F32),
-        in_specs=[anyw, vmem, vmem, vmem, vmem, vmem, pl.BlockSpec(memory_space=pltpu.SMEM)],
+        in_specs=[hbm] * 7,
         out_specs=anyw,
         scratch_shapes=[
+            pltpu.VMEM((PLANES, FLAT), F32),
+            pltpu.VMEM((3, FACES, CELLS), F32),
+            pltpu.VMEM((1, CELLS), F32),
+            pltpu.VMEM((FACES, CELLS), jnp.int32),
+            pltpu.VMEM((FACES, CELLS), jnp.int32),
+            pltpu.SMEM((2, HALO), jnp.int32),
             pltpu.VMEM((PLANES, CELLS, FLAT), F32),
             pltpu.VMEM((2, PLANES, HALO, FLAT), F32),
             pltpu.VMEM((2, PLANES, HALO, FLAT), F32),
             pltpu.VMEM((PLANES + 2, CELLS, WIDE), F32),
             pltpu.VMEM((PLANES + 2, CELLS, WIDE), F32),
             pltpu.VMEM((PLANES, CELLS, FLAT), F32),
+            pltpu.VMEM((2, 2, CELLS, 4 * 128), F32),
             pltpu.VMEM((CELLS, FLAT), F32),
             pltpu.VMEM((CELLS, FLAT), F32),
             pltpu.VMEM((CELLS, FLAT), F32),
@@ -434,9 +533,10 @@
             pltpu.VMEM((2, VELS, 1, 256), F32),
             dma((PLANES,)), dma((PLANES,)), dma((2,)), dma((2,)),
             dma((VELS,)), dma((VELS,)), dma((2, VELS)), dma((2, VELS)), dma((2, 2)), dma((2, 2)),
+            dma((6,)), dma((2, 2, LANES)), dma((2, 2, LANES)), dma((2, 2)), dma((2, 2)),
         ],
         compiler_params=pltpu.CompilerParams(
-            collective_id=0, has_side_effects=True, vmem_limit_bytes=24 * 1024 * 1024
+            collective_id=0, has_side_effects=True, vmem_limit_bytes=63 * 1024 * 1024
         ),
     )(
         jnp.transpose(distribution, (1, 0, 2)), freestream, face_area, cell_volume.reshape(1, CELLS), neighbours,

time: 73.1 us -> 54.9 us (0.75)
  Pallas kernels: 67.1 us -> 53 us
  local copies, waits for them, and re-layouts: 5.3 us -> 1.8 us
    pallas_call x1, Pallas kernels: 67.1 us -> 53 us  [body(): pl.pallas_call(kernel, out_shape=jax.ShapeDtypeStruct((PLANES, CELLS, FLA...]
    unnamed x15 -> x1, local copies, waits for them, and re-layouts: 5.3 us -> 1.8 us
where the time goes in v2:
time: 54.9 us; the launch traced here: 54.8 us
  Pallas kernels  53 us (97%)
  local copies, waits for them, and re-layouts  1.8 us (3%)
    pallas_call x1, Pallas kernels, body(): pl.pallas_call(kernel, out_shape=jax.ShapeDtypeStruct((PLANES, CELLS, FLA...  53 us
    unnamed x1, local copies, waits for them, and re-layouts  1.8 us

profile of v2, /device:TPU:1, one launch (start us, length us, event | category | flops | bytes accessed | tf_op | source)
XLA Modules:
  0.0 54.8 jit_solution(14470113580106030964)
XLA Ops:
  0.0 53.0 %shard_map.73 = f32[3,16,2304]{2,1,0:T(8,128)} custom-call(f32[3,16,2304]{2,1,0:T(8,128)} %bitcast.4, f32[3,2304]{1,0:T(4,128)} %free_h.1, f32[3,6,16]{2,1,0:T(8,128)} %area_h.1, f32[1,16]{1,0:T(1,128)} %bitcast.5, s32[6,16]{1,0:T(8,128)} %nb_h.1, s32[6,16]{1,0:T(8,128)} %wall_h.1, s32[2,4]{1,0:T(2,128)} %send_h.1), custom_call_target="tpu_custom_call" | custom-call | tf_op jit(solution)/shard_map/pallas_call | solution.py:504
  53.0 1.8 %copy.9 = f32[16,3,2304]{2,0,1:T(8,128)} copy(f32[16,3,2304]{2,0,1:T(8,128)} %bitcast.3) | data formatting | bytes 884736

commit v3 on v2

v3 whole, which is shorter than its diff:
```python
import jax
import jax.numpy as jnp
import numpy as np
from jax import lax
from jax.experimental import pallas as pl
from jax.experimental.pallas import tpu as pltpu
from jax.sharding import PartitionSpec as P

NV = 48
FLAT = NV * NV
STEP = 0.25
DT = 0.02
RATE = 0.002
FACES = 6
HALO = 4
CELLS = 16
PLANES = 3
MARGIN = 128
WIDE = FLAT + 2 * MARGIN
VELS = 16
LANES = 4
PARTS = ((8, 12), (12, 15), (15, 18), (0, 8))
MESH = pl.DeviceIdType.MESH
F32 = jnp.float32
BF16 = jnp.bfloat16


PLANE_SUMS = 22
TIMES_X = (0, 1, 2, 6, 7, 9, 10, 12, 13, 15, 16, 18, 19, 20, 21)
TIMES_XX = (0, 6, 9, 12, 15, 18, 19, 20, 21)
X_FACE = tuple(range(18))
SENT = tuple(range(PLANE_SUMS)) + TIMES_X + TIMES_XX + X_FACE
AT_X, AT_XX, AT_FACE = 22, 37, 46
MOMENTS = (0, AT_X, 1, 2, AT_XX, 3, 4, AT_X + 1, AT_X + 2, 5)


def plane_sums(j, k):
    y, z = (j - (NV - 1) / 2.0) * STEP, (k - (NV - 1) / 2.0) * STEP
    one = np.ones_like(y)
    lo_y, hi_y, lo_z, hi_z = ((at == end).astype(np.float64) for at in (j, k) for end in (0, NV - 1))
    sums = [one, y, z, y * y, z * z, y * z]
    for face in (lo_y, hi_y):
        sums += [face, face * z, face * z * z]
    for face in (lo_z, hi_z):
        sums += [face, face * y, face * y * y]
    sums += [lo_y * lo_z, lo_y * hi_z, hi_y * lo_z, hi_y * hi_z]
    return np.stack(sums)


def two_parts(x):
    hi = x.astype(jnp.bfloat16)
    return hi, (x - hi.astype(np.float64)).astype(jnp.bfloat16)


def sum_weights():
    at = np.arange(FLAT)
    weights = plane_sums(at // NV, at % NV)[list(SENT)].T
    return np.concatenate(two_parts(weights), axis=1)


def stencil_moments():
    line = np.array([0, 1, 2, 17, 23, 30, 45, 46, 47])
    at = np.stack(np.meshgrid(line, line, line, indexing="ij")).reshape(3, -1)

    def velocity(index):
        return (index - (NV - 1) / 2.0) * STEP

    planes = plane_sums(at[1], at[2])
    x = velocity(at[0])
    basis = [planes[c] for c in range(PLANE_SUMS)] + [planes[c] * x for c in TIMES_X] + [planes[c] * x * x for c in TIMES_XX]
    for end in (0, NV - 1):
        basis += [planes[c] * (at[0] == end) for c in X_FACE]

    def polynomials(index):
        v = velocity(index)
        inside = np.all((index >= 0) & (index < NV), axis=0)
        vx, vy, vz = v
        return np.stack([np.ones_like(vx), vx, vy, vz, vx * vx, vy * vy, vz * vz, vx * vy, vx * vz, vy * vz]) * inside

    def moved(*steps):
        index = at.copy()
        for axis, step in steps:
            index[axis] += step
        return polynomials(index)

    v = velocity(at)
    first = [(moved((i, -1)) - moved((i, 1))) / (2 * STEP) for i in range(3)]
    terms = [sum(v[i] * first[i] for i in range(3))] + first
    terms += [(moved((i, -1)) - 2 * moved() + moved((i, 1))) / STEP**2 for i in range(3)]
    for i, j in ((0, 1), (0, 2), (1, 2)):
        corner = {(p, q): moved((i, p), (j, q)) for p in (-1, 1) for q in (-1, 1)}
        terms.append((corner[-1, -1] - corner[-1, 1] - corner[1, -1] + corner[1, 1]) / (2 * STEP**2))
    wanted = np.concatenate(terms)
    found = np.linalg.lstsq(np.stack(basis).T, wanted.T, rcond=None)[0]
    found = np.round(found * 1024) / 1024
    assert np.abs(np.stack(basis).T @ found - wanted.T).max() < 1e-6
    out = np.zeros((128, 100))
    out[: len(basis)] = found
    return out


def small_matrices():
    row = np.arange(128)[:, None]
    col = np.arange(1280)[None, :] // 128
    ratios = row // 16 == col[:, :768]
    moments = row == np.array(MOMENTS)[col]
    products = (row % 10 == col) & (row < 110)
    stencil = np.zeros((128, 128))
    stencil[:, :100] = stencil_moments()
    for m, lane in enumerate(MOMENTS):
        stencil[lane, 100 + m] = 1.0
    plain = [a.astype(jnp.bfloat16) for a in (ratios, moments, products)]
    whole = np.concatenate(plain + list(two_parts(stencil)), axis=1)
    return np.concatenate(np.split(whole, whole.shape[1] // 128, axis=1), axis=0)


def split2(x):
    hi = x.astype(BF16)
    return hi, (x - hi.astype(F32)).astype(BF16)


def split3(x):
    hi = x.astype(BF16)
    r = x - hi.astype(F32)
    mid = r.astype(BF16)
    return hi, mid, (r - mid.astype(F32)).astype(BF16)


def lane_sums(acc):
    ones = jnp.ones((16, 128), BF16)
    total = None
    for part in split3(acc):
        term = lax.dot_general(ones, part, (((1,), (1,)), ((), ())), preferred_element_type=F32)
        total = term if total is None else total + term
    return total[0:1]


def times(x, matrix):
    out = jnp.dot(jnp.concatenate(split3(x), axis=0), matrix, preferred_element_type=F32)
    return out[0:16] + out[16:32] + out[32:48]


def spread(row, matrix):
    lane = lax.broadcasted_iota(jnp.int32, (CELLS, 128), 1)
    cell = lax.broadcasted_iota(jnp.int32, (CELLS, 128), 0)
    own = jnp.where((lane & (CELLS - 1)) == cell, jnp.broadcast_to(row, (CELLS, 128)), 0.0)
    return times(own, matrix)


def columns(matrix, first, count):
    return jnp.concatenate([matrix[128 * i : 128 * i + 128, :] for i in range(first, first + count)], axis=1)


def rep(x, n):
    return jnp.concatenate([x] * n, axis=1)


def kernel(
    dist, free_h, area_h, vol_h, nb_h, wall_h, send_h, wts_h, mat_h, out,
    free, area, vol, nb, wall, send, distv, hs, hr, wts, mat, pb, fa, wb, fb, fc, relay,
    yt, zt, mt, prm, sb, lhs, fsend, frecv, mrecv,
    in_sem, out_sem, h_ssem, h_rsem, f_ssem, f_rsem, m_ssem, m_rsem, p_ssem, p_rsem,
    s_sem, z_ssem, z_rsem, r_ssem, r_rsem,
):
    space = lax.axis_index("space")
    vel = lax.axis_index("vel")
    blocks = lax.axis_size("space")
    has_below, has_above = space > 0, space < blocks - 1
    has_left, has_right = vel > 0, vel < VELS - 1

    loads = [pltpu.make_async_copy(dist.at[p], distv.at[p], in_sem.at[p]) for p in range(PLANES)]
    small = [
        pltpu.make_async_copy(src, dst, s_sem.at[i])
        for i, (src, dst) in enumerate(
            ((area_h, area), (nb_h, nb), (wall_h, wall), (vol_h, vol), (send_h, send), (free_h, free))
        )
    ]
    late = [
        pltpu.make_async_copy(src, dst, s_sem.at[6 + i]) for i, (src, dst) in enumerate(((wts_h, wts), (mat_h, mat)))
    ]
    for copy in small + loads + late:
        copy.start()

    barrier = pltpu.get_barrier_semaphore()
    for d in range(1, VELS):
        pl.semaphore_signal(barrier, 1, device_id=(space, lax.rem(vel + d, VELS)), device_id_type=MESH)

    @pl.when(has_below)
    def _():
        pl.semaphore_signal(barrier, 1, device_id=(space - 1, vel), device_id_type=MESH)

    @pl.when(has_above)
    def _():
        pl.semaphore_signal(barrier, 1, device_id=(space + 1, vel), device_id_type=MESH)

    flat = lax.broadcasted_iota(jnp.int32, (CELLS, FLAT), 1).astype(F32)
    row = jnp.floor((flat + 0.5) / NV)
    y = (row - (NV - 1) / 2.0) * STEP
    z = (flat - row * NV - (NV - 1) / 2.0) * STEP
    yt[...] = y
    zt[...] = z
    mt[...] = jnp.exp(-(y * y + z * z) / 2.0)
    for buf, count in ((fa, PLANES + 4), (fb, PLANES + 2)):
        for plane in range(count):
            buf[plane, :, 0:MARGIN] = jnp.zeros((CELLS, MARGIN), F32)
            buf[plane, :, MARGIN + FLAT :] = jnp.zeros((CELLS, MARGIN), F32)

    @pl.when(jnp.logical_not(has_left))
    def _():
        for plane in (fa.at[0], fa.at[1], fb.at[0]):
            plane[...] = jnp.zeros((CELLS, WIDE), F32)

    @pl.when(jnp.logical_not(has_right))
    def _():
        for plane in (fa.at[PLANES + 2], fa.at[PLANES + 3], fb.at[PLANES + 1]):
            plane[...] = jnp.zeros((CELLS, WIDE), F32)

    for copy in small:
        copy.wait()

    prm[...] = jnp.zeros((32, 128), F32)
    for i in range(3):
        prm[6 * i : 6 * i + 6, 0:CELLS] = area[i]
    prm[18:24, 0:CELLS] = nb[...].astype(F32)
    prm[24:30, 0:CELLS] = wall[...].astype(F32)
    prm[30:31, 0:CELLS] = DT / vol[...]
    cols = prm[...].T[0:CELLS]
    for r in range(31):
        sb[r] = jnp.broadcast_to(cols[:, r : r + 1], (CELLS, 128))
    lane = lax.broadcasted_iota(jnp.int32, (CELLS, 64), 1) & 31
    for s in range(FACES):
        inside = (lane.astype(F32) == sb[18 + s][:, 0:64]) & (sb[24 + s][:, 0:64] < 0.5)
        lhs[16 * s : 16 * s + 16, :] = jnp.where(inside, 1.0, 0.0).astype(BF16)

    for copy in loads:
        copy.wait()
    for p in range(PLANES):
        for side in range(2):
            for r in range(HALO):
                hs[side, p, r : r + 1, :] = distv[p, pl.ds(send[side, r], 1), :]

    xs = {p: ((vel * PLANES + p).astype(F32) - (NV - 1) / 2.0) * STEP for p in range(-2, PLANES + 2)}
    mx = {p: jnp.exp(jnp.full((CELLS, 128), -0.5, F32) * (x * x)) for p, x in xs.items()}

    def gather_copy(src, dst, ssem, rsem, d):
        return pltpu.make_async_remote_copy(
            src_ref=src, dst_ref=dst.at[d], send_sem=ssem.at[d], recv_sem=rsem.at[d],
            device_id=(space, lax.rem(vel + d, VELS)), device_id_type=MESH,
        )

    def total(src, dst, ssem, rsem):
        acc = src[...]
        for d in range(1, VELS):
            gather_copy(src, dst, ssem, rsem, d).wait_recv()
            acc = acc + dst[d]
        return acc

    def flux_plane(p, carry):
        sx = [sb[s] * xs[p] for s in range(FACES)]

        def step(t, carry):
            off = pl.multiple_of(t * 256, 128)
            outs, ins = list(carry[:FACES]), list(carry[FACES:])
            for j in range(2):
                o = pl.ds(off + 128 * j, 128)
                dd, yy, zz = distv[p, :, o], yt[:, o], zt[:, o]
                mm = mt[:, o] * mx[p]
                for s in range(FACES):
                    w = jnp.maximum(sx[s] + sb[6 + s] * yy + sb[12 + s] * zz, 0.0)
                    outs[s] = outs[s] + w * dd
                    ins[s] = ins[s] + w * mm
            return tuple(outs + ins)

        return lax.fori_loop(0, FLAT // 256, step, carry)

    carry = tuple(jnp.zeros((CELLS, 128), F32) for _ in range(2 * FACES))
    for p in range(PLANES):
        carry = flux_plane(p, carry)
    fsend[0:1, 0:96] = lane_sums(jnp.concatenate(carry[:FACES], axis=0))
    fsend[0:1, 128:224] = lane_sums(jnp.concatenate(carry[FACES:], axis=0))
    fsend[0:1, 96:128] = jnp.zeros((1, 32), F32)
    fsend[0:1, 224:256] = jnp.ones((1, 32), F32)
    peers = VELS - 1 + has_below.astype(jnp.int32) + has_above.astype(jnp.int32)
    pl.semaphore_wait(barrier, peers)

    def halo(side, target):
        return pltpu.make_async_remote_copy(
            src_ref=hs.at[side], dst_ref=hr.at[1 - side], send_sem=h_ssem.at[side], recv_sem=h_rsem.at[1 - side],
            device_id=(target, vel), device_id_type=MESH,
        )

    @pl.when(has_above)
    def _():
        halo(1, space + 1).start()

    @pl.when(has_below)
    def _():
        halo(0, space - 1).start()

    @pl.when(jnp.logical_not(has_below))
    def _():
        for p in range(PLANES):
            hr[0, p] = jnp.broadcast_to(free[p : p + 1, :], (HALO, FLAT))

    @pl.when(jnp.logical_not(has_above))
    def _():
        for p in range(PLANES):
            hr[1, p] = jnp.broadcast_to(free[p : p + 1, :], (HALO, FLAT))

    for d in range(1, VELS):
        gather_copy(fsend, frecv, f_ssem, f_rsem, d).start()
    @pl.when(has_below)
    def _():
        halo(1, space + 1).wait_recv()

    @pl.when(has_above)
    def _():
        halo(0, space - 1).wait_recv()

    y_at, z_at = lax.rem(vel, LANES), vel // LANES

    def sides(right):
        return (LANES - 1, 0, 1, z_at < LANES - 1) if right else (0, LANES - 1, -1, z_at > 0)

    def ends(right):
        return (pl.ds(1, 2), pl.ds(0, 2)) if right else (pl.ds(0, 2), pl.ds(PLANES + 2, 2))

    def lanes_of(right, q):
        first, last = PARTS[q if right else LANES - 1 - q]
        return first, last - first

    def near_copy(right):
        src, dst = ends(right)
        i = 1 if right else 0
        return pltpu.make_async_remote_copy(
            src_ref=pb.at[src], dst_ref=fa.at[dst, :, pl.ds(MARGIN, FLAT)], send_sem=p_ssem.at[i], recv_sem=p_rsem.at[i],
            device_id=(space, vel + 1 if right else vel - 1), device_id_type=MESH,
        )

    def part_copy(right, q):
        home, other, dz, _ = sides(right)
        src, dst = ends(right)
        first, count = lanes_of(right, q)
        lanes, wide = pl.ds(128 * first, 128 * count), pl.ds(MARGIN + 128 * first, 128 * count)
        i = 1 if right else 0
        if q == home:
            dst_ref, recv, to = fa.at[dst, :, wide], z_rsem.at[i, q], (z_at + dz) * LANES + other
        else:
            dst_ref, recv, to = relay.at[i, :, :, pl.ds(0, 128 * count)], r_rsem.at[i], z_at * LANES + q
        return pltpu.make_async_remote_copy(
            src_ref=pb.at[src, :, lanes], dst_ref=dst_ref, send_sem=z_ssem.at[i, q], recv_sem=recv,
            device_id=(space, to), device_id_type=MESH,
        )

    def relay_copy(right, q):
        home, other, dz, _ = sides(right)
        src, dst = ends(right)
        first, count = lanes_of(right, q)
        lanes, wide = pl.ds(128 * first, 128 * count), pl.ds(MARGIN + 128 * first, 128 * count)
        i = 1 if right else 0
        return pltpu.make_async_remote_copy(
            src_ref=relay.at[i, :, :, pl.ds(0, 128 * count)], dst_ref=fa.at[dst, :, wide],
            send_sem=r_ssem.at[i], recv_sem=z_rsem.at[i, q],
            device_id=(space, (z_at + dz) * LANES + other), device_id_type=MESH,
        )

    def send_plane(right):
        home, _, _, inner = sides(right)

        @pl.when(y_at != home)
        def _():
            near_copy(right).start()

        @pl.when((y_at == home) & inner)
        def _():
            for q in range(LANES):
                part_copy(right, q).start()

    def pass_on():
        for right in (True, False):
            home, _, _, inner = sides(right)
            for q in range(LANES):
                if q != home:

                    @pl.when((y_at == q) & inner)
                    def _():
                        part_copy(right, q).wait_recv()
                        relay_copy(right, q).start()

    def recv_planes():
        for right in (True, False):
            home, other, _, _ = sides(right)
            from_z = z_at > 0 if right else z_at < LANES - 1

            @pl.when(y_at != other)
            def _():
                near_copy(right).wait_recv()

            @pl.when((y_at == other) & from_z)
            def _():
                for q in range(LANES):
                    if q == home:
                        part_copy(right, q).wait_recv()
                    else:
                        relay_copy(right, q).wait_recv()

    def end_planes():
        for right in (True, False):
            home, _, _, inner = sides(right)

            @pl.when(y_at != home)
            def _():
                near_copy(right).wait_send()

            @pl.when((y_at == home) & inner)
            def _():
                for q in range(LANES):
                    part_copy(right, q).wait_send()

            for q in range(LANES):
                if q != home:

                    @pl.when((y_at == q) & inner)
                    def _():
                        relay_copy(right, q).wait_send()

    def flow_plane(p):
        sx = [sb[s] * xs[p] for s in range(FACES)]
        scale = sb[30]

        def step(t, acc):
            off = pl.multiple_of(t * 256, 128)
            o = pl.ds(off, 256)
            ext = jnp.concatenate([distv[p, :, o], hr[0, p, :, o], hr[1, p, :, o], jnp.zeros((8, 256), F32)], axis=0)
            picked = jnp.dot(lhs[...], jnp.concatenate(split2(ext), axis=0), preferred_element_type=F32)
            for j in range(2):
                o = pl.ds(off + 128 * j, 128)
                dd, yy, zz = distv[p, :, o], yt[:, o], zt[:, o]
                out_sum, in_sum = None, None
                for s in range(FACES):
                    w = sx[s] + sb[6 + s] * yy + sb[12 + s] * zz
                    up = jnp.maximum(w, 0.0)
                    term = (w - up) * picked[16 * s : 16 * s + 16, 128 * j : 128 * j + 128]
                    out_sum = up if s == 0 else out_sum + up
                    in_sum = term if s == 0 else in_sum + term
                pb[p, :, o] = dd - scale * (out_sum * dd + in_sum)
            return acc

        lax.fori_loop(0, FLAT // 256, step, 0, unroll=True)

    flow_plane(1)
    flow_plane(0)
    send_plane(False)
    flow_plane(2)
    send_plane(True)

    for copy in late:
        copy.wait()

    flux = total(fsend, frecv, f_ssem, f_rsem)
    ratio = spread(flux[:, 0:128] / jnp.where(flux[:, 128:256] > 0.0, flux[:, 128:256], 1.0), columns(mat, 0, 6))
    for s in range(FACES):
        sb[18 + s] = jnp.where(sb[24 + s] > 0.5, -sb[30] * ratio[:, 128 * s : 128 * s + 128], 0.0)

    def wall_planes(off, planes):
        o = pl.ds(off, 128)
        yy, zz, mm = yt[:, o], zt[:, o], mt[:, o]
        sums = [None] * len(planes)
        for s in range(FACES):
            along = sb[6 + s] * yy + sb[12 + s] * zz
            for i, p in enumerate(planes):
                term = jnp.minimum(sb[s] * xs[p] + along, 0.0) * sb[18 + s]
                sums[i] = term if s == 0 else sums[i] + term
        return [sums[i] * (mm * mx[p]) for i, p in enumerate(planes)]

    def add_walls(t, acc):
        off = pl.multiple_of(t * 256, 128)
        halves = []
        for j in range(2):
            walls = wall_planes(off + 128 * j, range(PLANES))
            now = [pb[p, :, pl.ds(off + 128 * j, 128)] + walls[p] for p in range(PLANES)]
            for p in range(PLANES):
                fa[p + 2, :, pl.ds(off + 128 * j + MARGIN, 128)] = now[p]
            halves.append(jnp.concatenate(now, axis=0))
        parts = jnp.concatenate(split3(jnp.concatenate(halves, axis=1)), axis=0)
        return acc + jnp.dot(parts, wts[pl.ds(off, 256), :], preferred_element_type=F32)

    rows = PLANES * CELLS
    acc = lax.fori_loop(0, FLAT // 256, add_walls, jnp.zeros((3 * rows, 128), F32), unroll=True)
    acc = acc[0:rows] + acc[rows : 2 * rows] + acc[2 * rows :]
    acc = acc + pltpu.roll(acc, 64, 1)
    lane = lax.broadcasted_iota(jnp.int32, (CELLS, 128), 1) & 63
    sent = None
    for p in range(PLANES):
        face = 0.0
        if p == 0:
            face = jnp.where(has_left, 0.0, 1.0)
        if p == PLANES - 1:
            face = jnp.where(has_right, 0.0, 1.0)
        weight = jnp.where(
            lane < AT_X, 1.0, jnp.where(lane < AT_XX, xs[p], jnp.where(lane < AT_FACE, xs[p] * xs[p], face))
        )
        term = weight * acc[CELLS * p : CELLS * p + CELLS]
        sent = term if p == 0 else sent + term
    low = lax.broadcasted_iota(jnp.int32, (8, 128), 1) < 64
    mrecv[0] = jnp.where(low, sent[0:8], sent[8:16])
    for d in range(1, VELS):
        gather_copy(mrecv.at[0], mrecv, m_ssem, m_rsem, d).start()

    halo_planes = (-2, -1, PLANES, PLANES + 1)

    def halo_walls(t, acc):
        off = pl.multiple_of(t * 128, 128)
        walls = wall_planes(off, halo_planes)
        for i in range(4):
            wb[i, :, pl.ds(off, 128)] = walls[i]
        return acc

    pass_on()
    lax.fori_loop(0, FLAT // 128, halo_walls, 0, unroll=3)

    for d in range(1, VELS):
        gather_copy(mrecv.at[0], mrecv, m_ssem, m_rsem, d).wait_recv()
    packed = mrecv[0]
    for d in range(1, VELS):
        packed = packed + mrecv[d]

    def unpack(x):
        return jnp.concatenate([x, pltpu.roll(x, 64, 1)], axis=0)

    lane = lax.broadcasted_iota(jnp.int32, (CELLS, 128), 1)
    on_face = (lane >= AT_FACE) & (lane < 64)
    least = unpack(mrecv[vel])
    largest = unpack(mrecv[lax.rem(vel + 1, VELS)])
    sums = jnp.where(lane < AT_FACE, unpack(packed), jnp.where(on_face, least, 0.0))
    sums = sums + pltpu.roll(jnp.where(on_face, largest, 0.0), len(X_FACE), 1)

    def coefficients(allm):
        m = [allm[:, 128 * i : 128 * i + 128] for i in range(10)]
        inv = 1.0 / m[0]
        ux, uy, uz = m[1] * inv, m[2] * inv, m[3] * inv
        cxx, cyy, czz = m[4] * inv - ux * ux, m[5] * inv - uy * uy, m[6] * inv - uz * uz
        cxy, cxz, cyz = m[7] * inv - ux * uy, m[8] * inv - ux * uz, m[9] * inv - uy * uz
        theta = (cxx + cyy + czz) / 3.0
        a = (RATE * STEP**3) * m[0] * jnp.exp(0.19 * jnp.log(theta))
        lx, ly, lz = 0.5 * (theta + cxx), 0.5 * (theta + cyy), 0.5 * (theta + czz)
        terms = (a, -a * ux, -a * uy, -a * uz, a * lx, a * ly, a * lz, 0.5 * a * cxy, 0.5 * a * cxz, 0.5 * a * cyz)
        return terms, dict(
            ux=ux, a=a, k0=1.0 - 32.0 * a * (lx + ly + lz), lx=16.0 * a * lx,
            ys=a * (16.0 * ly + 0.5), a2=2.0 * a, a2uy=2.0 * a * uy, a2uz=2.0 * a * uz, zq=16.0 * a * lz,
            gxy=4.0 * a * cxy, gxz=4.0 * a * cxz, gyz=4.0 * a * cyz,
        )

    terms, c1 = coefficients(times(sums, columns(mat, 6, 10)))
    factor = jnp.where(lane < 110, 1.0, 0.0)
    for t in range(10):
        factor = jnp.where((lane >= 10 * t) & (lane < 10 * t + 10), terms[t], factor)
    stencil = times(sums, columns(mat, 26, 2))
    _, c2 = coefficients(times(factor * (stencil[:, 0:128] + stencil[:, 128:256]), columns(mat, 16, 10)))

    width = 768

    def relax_plane(src, at, dst, dst_at, p, c):
        n = width // 128
        margin = MARGIN if dst.shape[-1] == WIDE else 0
        drift_n = c["a2"] * (xs[p] + STEP - c["ux"]) + c["lx"]
        drift_p = c["lx"] - c["a2"] * (xs[p] - STEP - c["ux"])
        kn, kp, k0 = rep(drift_n, n), rep(drift_p, n), rep(c["k0"], n)
        ys, a2, a2uy, a2uz, zq = (rep(c[q], n) for q in ("ys", "a2", "a2uy", "a2uz", "zq"))
        gxy, gxz, gyz = (rep(c[q], n) for q in ("gxy", "gxz", "gyz"))

        def step(t, acc):
            off = pl.multiple_of(t * width, 128)
            win = pl.ds(off, width + 2 * MARGIN)
            cen = pl.ds(off, width)
            cw, nw, pw = src[at, :, win], src[at + 1, :, win], src[at - 1, :, win]
            xw = nw - pw
            yy, zz = yt[:, cen], zt[:, cen]
            total_w = width + 2 * MARGIN

            def up(v):
                return pltpu.roll(v, total_w - NV, 1)[:, MARGIN : MARGIN + width]

            def down(v):
                return pltpu.roll(v, NV, 1)[:, MARGIN : MARGIN + width]

            cc, nn, pp = (v[:, MARGIN : MARGIN + width] for v in (cw, nw, pw))
            u, d = up(cw), down(cw)
            diff = u - d
            res = k0 * cc + kn * nn + kp * pp
            res = res + ys * (u + d) + (a2 * yy - a2uy) * diff + gxy * (up(xw) - down(xw))
            cross = gxz * (nn - pp) + gyz * diff
            zr = a2 * zz - a2uz
            plus = (zq + zr) * cc + cross
            minus = (zq - zr) * cc - cross
            edge = (NV - 1) / 2.0 * STEP
            res = res + jnp.where(zz < edge - 0.1, pltpu.roll(plus, width - 1, 1), 0.0)
            res = res + jnp.where(zz > 0.1 - edge, pltpu.roll(minus, 1, 1), 0.0)
            dst[dst_at, :, pl.ds(off + margin, width)] = res
            return acc

        lax.fori_loop(0, FLAT // width, step, 0, unroll=True)

    relax_plane(fa, 3, fb, 2, 1, c1)
    recv_planes()

    @pl.when(has_left)
    def _():
        for i in range(2):
            fa[i, :, MARGIN : MARGIN + FLAT] = fa[i, :, MARGIN : MARGIN + FLAT] + wb[i]
        relax_plane(fa, 1, fb, 0, -1, c1)

    @pl.when(has_right)
    def _():
        for i in range(2):
            plane = PLANES + 2 + i
            fa[plane, :, MARGIN : MARGIN + FLAT] = fa[plane, :, MARGIN : MARGIN + FLAT] + wb[2 + i]
        relax_plane(fa, PLANES + 2, fb, PLANES + 1, PLANES, c1)

    relax_plane(fa, 2, fb, 1, 0, c1)
    relax_plane(fa, 4, fb, 3, 2, c1)
    stores = [pltpu.make_async_copy(fc.at[p], out.at[p], out_sem.at[p]) for p in range(PLANES)]
    for p in range(PLANES):
        relax_plane(fb, p + 1, fc, p, p, c2)
        stores[p].start()

    @pl.when(has_above)
    def _():
        halo(1, space + 1).wait_send()

    @pl.when(has_below)
    def _():
        halo(0, space - 1).wait_send()

    for d in range(1, VELS):
        gather_copy(fsend, frecv, f_ssem, f_rsem, d).wait_send()
        gather_copy(mrecv.at[0], mrecv, m_ssem, m_rsem, d).wait_send()
    end_planes()
    for copy in stores:
        copy.wait()


def body(distribution, freestream, face_area, cell_volume, neighbours, wall_flags, send_cells):
    dma = pltpu.SemaphoreType.DMA
    hbm = pl.BlockSpec(memory_space=pltpu.HBM)
    anyw = pl.BlockSpec(memory_space=pl.ANY)
    new = pl.pallas_call(
        kernel,
        out_shape=jax.ShapeDtypeStruct((PLANES, CELLS, FLAT), F32),
        in_specs=[hbm] * 9,
        out_specs=anyw,
        scratch_shapes=[
            pltpu.VMEM((PLANES, FLAT), F32),
            pltpu.VMEM((3, FACES, CELLS), F32),
            pltpu.VMEM((1, CELLS), F32),
            pltpu.VMEM((FACES, CELLS), jnp.int32),
            pltpu.VMEM((FACES, CELLS), jnp.int32),
            pltpu.SMEM((2, HALO), jnp.int32),
            pltpu.VMEM((PLANES, CELLS, FLAT), F32),
            pltpu.VMEM((2, PLANES, HALO, FLAT), F32),
            pltpu.VMEM((2, PLANES, HALO, FLAT), F32),
            pltpu.VMEM((FLAT, 128), BF16),
            pltpu.VMEM((28 * 128, 128), BF16),
            pltpu.VMEM((PLANES, CELLS, FLAT), F32),
            pltpu.VMEM((PLANES + 4, CELLS, WIDE), F32),
            pltpu.VMEM((4, CELLS, FLAT), F32),
            pltpu.VMEM((PLANES + 2, CELLS, WIDE), F32),
            pltpu.VMEM((PLANES, CELLS, FLAT), F32),
            pltpu.VMEM((2, 2, CELLS, 4 * 128), F32),
            pltpu.VMEM((CELLS, FLAT), F32),
            pltpu.VMEM((CELLS, FLAT), F32),
            pltpu.VMEM((CELLS, FLAT), F32),
            pltpu.VMEM((32, 128), F32),
            pltpu.VMEM((32, CELLS, 128), F32),
            pltpu.VMEM((96, 64), BF16),
            pltpu.VMEM((1, 256), F32),
            pltpu.VMEM((VELS, 1, 256), F32),
            pltpu.VMEM((VELS, 8, 128), F32),
            dma((PLANES,)), dma((PLANES,)), dma((2,)), dma((2,)),
            dma((VELS,)), dma((VELS,)), dma((VELS,)), dma((VELS,)), dma((2,)), dma((2,)),
            dma((8,)), dma((2, LANES)), dma((2, LANES)), dma((2,)), dma((2,)),
        ],
        compiler_params=pltpu.CompilerParams(
            collective_id=0, has_side_effects=True, vmem_limit_bytes=63 * 1024 * 1024
        ),
    )(
        jnp.transpose(distribution, (1, 0, 2)), freestream, face_area, cell_volume.reshape(1, CELLS), neighbours,
        wall_flags, send_cells, jnp.asarray(sum_weights()), jnp.asarray(small_matrices()),
    )
    return jnp.transpose(new, (1, 0, 2))


def solution(mesh):
    in_specs = (
        P("space", "vel", None),
        P("vel", None),
        P(None, None, "space"),
        P("space"),
        P(None, "space"),
        P(None, "space"),
        P(None, "space"),
    )
    out_specs = P("space", "vel", None)
    return jax.shard_map(body, mesh=mesh, in_specs=in_specs, out_specs=out_specs, check_vma=False)
```

time: 54.9 us -> 45.9 us (0.84)
  Pallas kernels: 53 us -> 43.9 us
    pallas_call x1, Pallas kernels: 53 us -> 43.9 us  [body(): pl.pallas_call(kernel, out_shape=jax.ShapeDtypeStruct((PLANES, CELLS, FLA...]
where the time goes in v3:
time: 45.9 us; the launch traced here: 45.7 us
  Pallas kernels  43.9 us (96%)
  local copies, waits for them, and re-layouts  1.8 us (4%)
    pallas_call x1, Pallas kernels, body(): pl.pallas_call(kernel, out_shape=jax.ShapeDtypeStruct((PLANES, CELLS, FLA...  43.9 us
    unnamed x1, local copies, waits for them, and re-layouts  1.8 us

profile of v3, /device:TPU:1, one launch (start us, length us, event | category | flops | bytes accessed | tf_op | source)
XLA Modules:
  0.0 45.7 jit_solution(8713078110234808715)
XLA Ops:
  0.0 43.9 %shard_map.91 = f32[3,16,2304]{2,1,0:T(8,128)} custom-call(f32[3,16,2304]{2,1,0:T(8,128)} %bitcast.4, f32[3,2304]{1,0:T(4,128)} %free_h.1, f32[3,6,16]{2,1,0:T(8,128)} %area_h.1, f32[1,16]{1,0:T(1,128)} %bitcast.5, s32[6,16]{1,0:T(8,128)} %nb_h.1, s32[6,16]{1,0:T(8,128)} %wall_h.1, s32[2,4]{1,0:T(2,128)} %send_h.1, bf16[2304,128]{1,0:T(8,128)(2,1)} %constant.4.clone.wts_h, ...), custom_call_target="tpu_custom_call" | custom-call | tf_op jit(solution)/shard_map/pallas_call | solution.py:647
  43.9 1.8 %copy.11 = f32[16,3,2304]{2,0,1:T(8,128)} copy(f32[16,3,2304]{2,0,1:T(8,128)} %bitcast.3) | data formatting | bytes 884736

commit v4 on v3

--- a/solution.py
+++ b/solution.py
@@ -18,6 +18,7 @@
 MARGIN = 128
 WIDE = FLAT + 2 * MARGIN
 VELS = 16
+WALL_ROWS = FACES * PLANES * CELLS
 LANES = 4
 PARTS = ((8, 12), (12, 15), (15, 18), (0, 8))
 MESH = pl.DeviceIdType.MESH
@@ -151,15 +152,18 @@
     return jnp.concatenate([matrix[128 * i : 128 * i + 128, :] for i in range(first, first + count)], axis=1)
 
 
+FAR_FIRST = sorted(range(1, VELS), key=lambda d: -min(d, VELS - d))
+
+
 def rep(x, n):
     return jnp.concatenate([x] * n, axis=1)
 
 
 def kernel(
     dist, free_h, area_h, vol_h, nb_h, wall_h, send_h, wts_h, mat_h, out,
-    free, area, vol, nb, wall, send, distv, hs, hr, wts, mat, pb, fa, wb, fb, fc, relay,
+    free, area, vol, nb, wall, send, distv, hs, hr, wts, mat, pb, fa, wb, fb, relay, qm, fq, pm,
     yt, zt, mt, prm, sb, lhs, fsend, frecv, mrecv,
-    in_sem, out_sem, h_ssem, h_rsem, f_ssem, f_rsem, m_ssem, m_rsem, p_ssem, p_rsem,
+    in_sem, h_ssem, h_rsem, f_ssem, f_rsem, m_ssem, m_rsem, p_ssem, p_rsem,
     s_sem, z_ssem, z_rsem, r_ssem, r_rsem,
 ):
     space = lax.axis_index("space")
@@ -182,7 +186,7 @@
         copy.start()
 
     barrier = pltpu.get_barrier_semaphore()
-    for d in range(1, VELS):
+    for d in FAR_FIRST:
         pl.semaphore_signal(barrier, 1, device_id=(space, lax.rem(vel + d, VELS)), device_id_type=MESH)
 
     @pl.when(has_below)
@@ -239,7 +243,10 @@
             for r in range(HALO):
                 hs[side, p, r : r + 1, :] = distv[p, pl.ds(send[side, r], 1), :]
 
-    xs = {p: ((vel * PLANES + p).astype(F32) - (NV - 1) / 2.0) * STEP for p in range(-2, PLANES + 2)}
+    def x_of(p):
+        return ((vel * PLANES + p).astype(F32) - (NV - 1) / 2.0) * STEP
+
+    xs = {p: x_of(p) for p in range(-2, PLANES + 2)}
     mx = {p: jnp.exp(jnp.full((CELLS, 128), -0.5, F32) * (x * x)) for p, x in xs.items()}
 
     def gather_copy(src, dst, ssem, rsem, d):
@@ -283,19 +290,25 @@
     peers = VELS - 1 + has_below.astype(jnp.int32) + has_above.astype(jnp.int32)
     pl.semaphore_wait(barrier, peers)
 
-    def halo(side, target):
+    def halo(side, p, target):
         return pltpu.make_async_remote_copy(
-            src_ref=hs.at[side], dst_ref=hr.at[1 - side], send_sem=h_ssem.at[side], recv_sem=h_rsem.at[1 - side],
+            src_ref=hs.at[side, p], dst_ref=hr.at[1 - side, p],
+            send_sem=h_ssem.at[side, p], recv_sem=h_rsem.at[1 - side, p],
             device_id=(target, vel), device_id_type=MESH,
         )
 
-    @pl.when(has_above)
-    def _():
-        halo(1, space + 1).start()
-
-    @pl.when(has_below)
-    def _():
-        halo(0, space - 1).start()
+    y_at, z_at = lax.rem(vel, LANES), vel // LANES
+    first = jnp.where(y_at == LANES - 1, PLANES - 1, 0)
+    order = (1, first, PLANES - 1 - first)
+    for p in order:
+
+        @pl.when(has_above)
+        def _():
+            halo(1, p, space + 1).start()
+
+        @pl.when(has_below)
+        def _():
+            halo(0, p, space - 1).start()
 
     @pl.when(jnp.logical_not(has_below))
     def _():
@@ -307,102 +320,117 @@
         for p in range(PLANES):
             hr[1, p] = jnp.broadcast_to(free[p : p + 1, :], (HALO, FLAT))
 
-    for d in range(1, VELS):
+    for d in FAR_FIRST:
         gather_copy(fsend, frecv, f_ssem, f_rsem, d).start()
-    @pl.when(has_below)
-    def _():
-        halo(1, space + 1).wait_recv()
-
-    @pl.when(has_above)
-    def _():
-        halo(0, space - 1).wait_recv()
-
-    y_at, z_at = lax.rem(vel, LANES), vel // LANES
+
+    for copy in late:
+        copy.wait()
+
+    def unit_walls(t, acc):
+        off = pl.multiple_of(t * 128, 128)
+        o = pl.ds(off, 128)
+        yy, zz, mm = yt[:, o], zt[:, o], mt[:, o]
+        for s in range(FACES):
+            along = sb[6 + s] * yy + sb[12 + s] * zz
+            for p in range(PLANES):
+                at = (s * PLANES + p) * CELLS
+                hi, lo = split2(jnp.minimum(sb[s] * xs[p] + along, 0.0) * (mm * mx[p]))
+                qm[at : at + CELLS, o] = hi
+                qm[WALL_ROWS + at : WALL_ROWS + at + CELLS, o] = lo
+        return acc
+
+    lax.fori_loop(0, FLAT // 128, unit_walls, 0, unroll=3)
+    unit = jnp.dot(qm[...], wts[...], preferred_element_type=F32)
+    fq[...] = unit[0:WALL_ROWS] + unit[WALL_ROWS:]
 
     def sides(right):
         return (LANES - 1, 0, 1, z_at < LANES - 1) if right else (0, LANES - 1, -1, z_at > 0)
 
-    def ends(right):
-        return (pl.ds(1, 2), pl.ds(0, 2)) if right else (pl.ds(0, 2), pl.ds(PLANES + 2, 2))
+    def ends(right, n):
+        return (1 + n, n) if right else (n, PLANES + 2 + n)
 
     def lanes_of(right, q):
-        first, last = PARTS[q if right else LANES - 1 - q]
-        return first, last - first
-
-    def near_copy(right):
-        src, dst = ends(right)
+        begin, last = PARTS[q if right else LANES - 1 - q]
+        return begin, last - begin
+
+    def near_copy(right, n):
+        src, dst = ends(right, n)
         i = 1 if right else 0
         return pltpu.make_async_remote_copy(
-            src_ref=pb.at[src], dst_ref=fa.at[dst, :, pl.ds(MARGIN, FLAT)], send_sem=p_ssem.at[i], recv_sem=p_rsem.at[i],
+            src_ref=pb.at[src], dst_ref=fa.at[dst, :, pl.ds(MARGIN, FLAT)],
+            send_sem=p_ssem.at[i, n], recv_sem=p_rsem.at[i, n],
             device_id=(space, vel + 1 if right else vel - 1), device_id_type=MESH,
         )
 
-    def part_copy(right, q):
+    def part_copy(right, n, q):
         home, other, dz, _ = sides(right)
-        src, dst = ends(right)
-        first, count = lanes_of(right, q)
-        lanes, wide = pl.ds(128 * first, 128 * count), pl.ds(MARGIN + 128 * first, 128 * count)
+        src, dst = ends(right, n)
+        begin, count = lanes_of(right, q)
+        lanes, wide = pl.ds(128 * begin, 128 * count), pl.ds(MARGIN + 128 * begin, 128 * count)
         i = 1 if right else 0
         if q == home:
-            dst_ref, recv, to = fa.at[dst, :, wide], z_rsem.at[i, q], (z_at + dz) * LANES + other
+            dst_ref, recv, to = fa.at[dst, :, wide], z_rsem.at[i, q, n], (z_at + dz) * LANES + other
         else:
-            dst_ref, recv, to = relay.at[i, :, :, pl.ds(0, 128 * count)], r_rsem.at[i], z_at * LANES + q
+            dst_ref, recv, to = relay.at[i, n, :, pl.ds(0, 128 * count)], r_rsem.at[i, n], z_at * LANES + q
         return pltpu.make_async_remote_copy(
-            src_ref=pb.at[src, :, lanes], dst_ref=dst_ref, send_sem=z_ssem.at[i, q], recv_sem=recv,
+            src_ref=pb.at[src, :, lanes], dst_ref=dst_ref, send_sem=z_ssem.at[i, q, n], recv_sem=recv,
             device_id=(space, to), device_id_type=MESH,
         )
 
-    def relay_copy(right, q):
+    def relay_copy(right, n, q):
         home, other, dz, _ = sides(right)
-        src, dst = ends(right)
-        first, count = lanes_of(right, q)
-        lanes, wide = pl.ds(128 * first, 128 * count), pl.ds(MARGIN + 128 * first, 128 * count)
+        src, dst = ends(right, n)
+        begin, count = lanes_of(right, q)
+        wide = pl.ds(MARGIN + 128 * begin, 128 * count)
         i = 1 if right else 0
         return pltpu.make_async_remote_copy(
-            src_ref=relay.at[i, :, :, pl.ds(0, 128 * count)], dst_ref=fa.at[dst, :, wide],
-            send_sem=r_ssem.at[i], recv_sem=z_rsem.at[i, q],
+            src_ref=relay.at[i, n, :, pl.ds(0, 128 * count)], dst_ref=fa.at[dst, :, wide],
+            send_sem=r_ssem.at[i, n], recv_sem=z_rsem.at[i, q, n],
             device_id=(space, (z_at + dz) * LANES + other), device_id_type=MESH,
         )
 
-    def send_plane(right):
+    def send_plane(right, n):
         home, _, _, inner = sides(right)
 
         @pl.when(y_at != home)
         def _():
-            near_copy(right).start()
+            near_copy(right, n).start()
 
         @pl.when((y_at == home) & inner)
         def _():
             for q in range(LANES):
-                part_copy(right, q).start()
+                part_copy(right, n, q).start()
 
     def pass_on():
-        for right in (True, False):
-            home, _, _, inner = sides(right)
-            for q in range(LANES):
-                if q != home:
-
-                    @pl.when((y_at == q) & inner)
-                    def _():
-                        part_copy(right, q).wait_recv()
-                        relay_copy(right, q).start()
-
-    def recv_planes():
-        for right in (True, False):
-            home, other, _, _ = sides(right)
-            from_z = z_at > 0 if right else z_at < LANES - 1
-
-            @pl.when(y_at != other)
-            def _():
-                near_copy(right).wait_recv()
-
-            @pl.when((y_at == other) & from_z)
-            def _():
+        for step in range(2):
+            for right in (True, False):
+                n = step if right else 1 - step
+                home, _, _, inner = sides(right)
+                for q in range(LANES):
+                    if q != home:
+
+                        @pl.when((y_at == q) & inner)
+                        def _():
+                            part_copy(right, n, q).wait_recv()
+                            relay_copy(right, n, q).start()
+
+    def recv_planes(right, when):
+        home, other, _, _ = sides(right)
+        from_z = z_at > 0 if right else z_at < LANES - 1
+
+        @pl.when((y_at != other) & when)
+        def _():
+            for n in range(2):
+                near_copy(right, n).wait_recv()
+
+        @pl.when((y_at == other) & from_z & when)
+        def _():
+            for n in range(2):
                 for q in range(LANES):
                     if q == home:
-                        part_copy(right, q).wait_recv()
+                        part_copy(right, n, q).wait_recv()
                     else:
-                        relay_copy(right, q).wait_recv()
+                        relay_copy(right, n, q).wait_recv()
 
     def end_planes():
         for right in (True, False):
@@ -410,22 +438,26 @@
 
             @pl.when(y_at != home)
             def _():
-                near_copy(right).wait_send()
+                for n in range(2):
+                    near_copy(right, n).wait_send()
 
             @pl.when((y_at == home) & inner)
             def _():
-                for q in range(LANES):
-                    part_copy(right, q).wait_send()
+                for n in range(2):
+                    for q in range(LANES):
+                        part_copy(right, n, q).wait_send()
 
             for q in range(LANES):
                 if q != home:
 
                     @pl.when((y_at == q) & inner)
                     def _():
-                        relay_copy(right, q).wait_send()
+                        for n in range(2):
+                            relay_copy(right, n, q).wait_send()
 
     def flow_plane(p):
-        sx = [sb[s] * xs[p] for s in range(FACES)]
+        x = x_of(p)
+        sx = [sb[s] * x for s in range(FACES)]
         scale = sb[30]
 
         def step(t, acc):
@@ -443,19 +475,41 @@
                     term = (w - up) * picked[16 * s : 16 * s + 16, 128 * j : 128 * j + 128]
                     out_sum = up if s == 0 else out_sum + up
                     in_sum = term if s == 0 else in_sum + term
-                pb[p, :, o] = dd - scale * (out_sum * dd + in_sum)
+                f = dd - scale * (out_sum * dd + in_sum)
+                pb[p, :, o] = f
+                for i, part in enumerate(split3(f)):
+                    pm[pl.ds(pl.multiple_of((i * PLANES + p) * CELLS, CELLS), CELLS), o] = part
             return acc
 
         lax.fori_loop(0, FLAT // 256, step, 0, unroll=True)
 
-    flow_plane(1)
-    flow_plane(0)
-    send_plane(False)
-    flow_plane(2)
-    send_plane(True)
-
-    for copy in late:
-        copy.wait()
+    for step, p in enumerate(order):
+
+        @pl.when(has_below)
+        def _():
+            halo(1, p, space + 1).wait_recv()
+
+        @pl.when(has_above)
+        def _():
+            halo(0, p, space - 1).wait_recv()
+
+        flow_plane(p)
+        if step == 0:
+            send_plane(True, 0)
+            send_plane(False, 1)
+        else:
+
+            @pl.when(p == PLANES - 1)
+            def _():
+                send_plane(True, 1)
+
+            @pl.when(p == 0)
+            def _():
+                send_plane(False, 0)
+
+    rows = PLANES * CELLS
+    flow = jnp.dot(pm[...], wts[...], preferred_element_type=F32)
+    flow = flow[0:rows] + flow[rows : 2 * rows] + flow[2 * rows :]
 
     flux = total(fsend, frecv, f_ssem, f_rsem)
     ratio = spread(flux[:, 0:128] / jnp.where(flux[:, 128:256] > 0.0, flux[:, 128:256], 1.0), columns(mat, 0, 6))
@@ -473,21 +527,14 @@
                 sums[i] = term if s == 0 else sums[i] + term
         return [sums[i] * (mm * mx[p]) for i, p in enumerate(planes)]
 
-    def add_walls(t, acc):
-        off = pl.multiple_of(t * 256, 128)
-        halves = []
-        for j in range(2):
-            walls = wall_planes(off + 128 * j, range(PLANES))
-            now = [pb[p, :, pl.ds(off + 128 * j, 128)] + walls[p] for p in range(PLANES)]
-            for p in range(PLANES):
-                fa[p + 2, :, pl.ds(off + 128 * j + MARGIN, 128)] = now[p]
-            halves.append(jnp.concatenate(now, axis=0))
-        parts = jnp.concatenate(split3(jnp.concatenate(halves, axis=1)), axis=0)
-        return acc + jnp.dot(parts, wts[pl.ds(off, 256), :], preferred_element_type=F32)
-
-    rows = PLANES * CELLS
-    acc = lax.fori_loop(0, FLAT // 256, add_walls, jnp.zeros((3 * rows, 128), F32), unroll=True)
-    acc = acc[0:rows] + acc[rows : 2 * rows] + acc[2 * rows :]
+    acc = []
+    for p in range(PLANES):
+        plane = flow[CELLS * p : CELLS * p + CELLS]
+        for s in range(FACES):
+            at = (s * PLANES + p) * CELLS
+            plane = plane + sb[18 + s] * fq[at : at + CELLS, :]
+        acc.append(plane)
+    acc = jnp.concatenate(acc, axis=0)
     acc = acc + pltpu.roll(acc, 64, 1)
     lane = lax.broadcasted_iota(jnp.int32, (CELLS, 128), 1) & 63
     sent = None
@@ -504,8 +551,17 @@
         sent = term if p == 0 else sent + term
     low = lax.broadcasted_iota(jnp.int32, (8, 128), 1) < 64
     mrecv[0] = jnp.where(low, sent[0:8], sent[8:16])
-    for d in range(1, VELS):
+    for d in FAR_FIRST:
         gather_copy(mrecv.at[0], mrecv, m_ssem, m_rsem, d).start()
+
+    def add_walls(t, acc):
+        off = pl.multiple_of(t * 128, 128)
+        walls = wall_planes(off, range(PLANES))
+        for p in range(PLANES):
+            fa[p + 2, :, pl.ds(off + MARGIN, 128)] = pb[p, :, pl.ds(off, 128)] + walls[p]
+        return acc
+
+    lax.fori_loop(0, FLAT // 128, add_walls, 0, unroll=3)
 
     halo_planes = (-2, -1, PLANES, PLANES + 1)
 
@@ -563,8 +619,9 @@
     def relax_plane(src, at, dst, dst_at, p, c):
         n = width // 128
         margin = MARGIN if dst.shape[-1] == WIDE else 0
-        drift_n = c["a2"] * (xs[p] + STEP - c["ux"]) + c["lx"]
-        drift_p = c["lx"] - c["a2"] * (xs[p] - STEP - c["ux"])
+        x = x_of(p)
+        drift_n = c["a2"] * (x + STEP - c["ux"]) + c["lx"]
+        drift_p = c["lx"] - c["a2"] * (x - STEP - c["ux"])
         kn, kp, k0 = rep(drift_n, n), rep(drift_p, n), rep(c["k0"], n)
         ys, a2, a2uy, a2uz, zq = (rep(c[q], n) for q in ("ys", "a2", "a2uy", "a2uz", "zq"))
         gxy, gxz, gyz = (rep(c[q], n) for q in ("gxy", "gxz", "gyz"))
@@ -602,53 +659,54 @@
         lax.fori_loop(0, FLAT // width, step, 0, unroll=True)
 
     relax_plane(fa, 3, fb, 2, 1, c1)
-    recv_planes()
-
-    @pl.when(has_left)
-    def _():
-        for i in range(2):
-            fa[i, :, MARGIN : MARGIN + FLAT] = fa[i, :, MARGIN : MARGIN + FLAT] + wb[i]
-        relax_plane(fa, 1, fb, 0, -1, c1)
-
-    @pl.when(has_right)
-    def _():
-        for i in range(2):
-            plane = PLANES + 2 + i
-            fa[plane, :, MARGIN : MARGIN + FLAT] = fa[plane, :, MARGIN : MARGIN + FLAT] + wb[2 + i]
-        relax_plane(fa, PLANES + 2, fb, PLANES + 1, PLANES, c1)
-
-    relax_plane(fa, 2, fb, 1, 0, c1)
-    relax_plane(fa, 4, fb, 3, 2, c1)
-    stores = [pltpu.make_async_copy(fc.at[p], out.at[p], out_sem.at[p]) for p in range(PLANES)]
-    for p in range(PLANES):
-        relax_plane(fb, p + 1, fc, p, p, c2)
-        stores[p].start()
+
+    def relax_side(right):
+        left = jnp.logical_not(right)
+        recv_planes(True, left)
+        recv_planes(False, right)
+        arrived = jnp.where(right, PLANES + 2, 0)
+        walls = jnp.where(right, 2, 0)
+        halo_at = jnp.where(right, PLANES + 2, 1)
+        edge_at = jnp.where(right, PLANES + 1, 2)
+
+        @pl.when((right & has_right) | (left & has_left))
+        def _():
+            for i in range(2):
+                fa[arrived + i, :, MARGIN : MARGIN + FLAT] = fa[arrived + i, :, MARGIN : MARGIN + FLAT] + wb[walls + i]
+            relax_plane(fa, halo_at, fb, halo_at - 1, halo_at - 2, c1)
+
+        relax_plane(fa, edge_at, fb, edge_at - 1, edge_at - 2, c1)
+        relax_plane(fb, edge_at - 1, out, edge_at - 2, edge_at - 2, c2)
+
+    right_first = y_at == 0
+    relax_side(right_first)
+    relax_side(jnp.logical_not(right_first))
+    relax_plane(fb, 2, out, 1, 1, c2)
 
     @pl.when(has_above)
     def _():
-        halo(1, space + 1).wait_send()
+        for p in range(PLANES):
+            halo(1, p, space + 1).wait_send()
 
     @pl.when(has_below)
     def _():
-        halo(0, space - 1).wait_send()
+        for p in range(PLANES):
+            halo(0, p, space - 1).wait_send()
 
     for d in range(1, VELS):
         gather_copy(fsend, frecv, f_ssem, f_rsem, d).wait_send()
         gather_copy(mrecv.at[0], mrecv, m_ssem, m_rsem, d).wait_send()
     end_planes()
-    for copy in stores:
-        copy.wait()
 
 
 def body(distribution, freestream, face_area, cell_volume, neighbours, wall_flags, send_cells):
     dma = pltpu.SemaphoreType.DMA
     hbm = pl.BlockSpec(memory_space=pltpu.HBM)
-    anyw = pl.BlockSpec(memory_space=pl.ANY)
     new = pl.pallas_call(
         kernel,
-        out_shape=jax.ShapeDtypeStruct((PLANES, CELLS, FLAT), F32),
+        out_shape=pltpu.VMEM((PLANES, CELLS, FLAT), F32),
         in_specs=[hbm] * 9,
-        out_specs=anyw,
+        out_specs=pl.BlockSpec(memory_space=pltpu.VMEM),
         scratch_shapes=[
             pltpu.VMEM((PLANES, FLAT), F32),
             pltpu.VMEM((3, FACES, CELLS), F32),
@@ -665,8 +723,10 @@
             pltpu.VMEM((PLANES + 4, CELLS, WIDE), F32),
             pltpu.VMEM((4, CELLS, FLAT), F32),
             pltpu.VMEM((PLANES + 2, CELLS, WIDE), F32),
-            pltpu.VMEM((PLANES, CELLS, FLAT), F32),
             pltpu.VMEM((2, 2, CELLS, 4 * 128), F32),
+            pltpu.VMEM((2 * FACES * PLANES * CELLS, FLAT), BF16),
+            pltpu.VMEM((FACES * PLANES * CELLS, 128), F32),
+            pltpu.VMEM((3 * PLANES * CELLS, FLAT), BF16),
             pltpu.VMEM((CELLS, FLAT), F32),
             pltpu.VMEM((CELLS, FLAT), F32),
             pltpu.VMEM((CELLS, FLAT), F32),
@@ -676,12 +736,12 @@
             pltpu.VMEM((1, 256), F32),
             pltpu.VMEM((VELS, 1, 256), F32),
             pltpu.VMEM((VELS, 8, 128), F32),
-            dma((PLANES,)), dma((PLANES,)), dma((2,)), dma((2,)),
-            dma((VELS,)), dma((VELS,)), dma((VELS,)), dma((VELS,)), dma((2,)), dma((2,)),
-            dma((8,)), dma((2, LANES)), dma((2, LANES)), dma((2,)), dma((2,)),
+            dma((PLANES,)), dma((2, PLANES)), dma((2, PLANES)),
+            dma((VELS,)), dma((VELS,)), dma((VELS,)), dma((VELS,)), dma((2, 2)), dma((2, 2)),
+            dma((8,)), dma((2, LANES, 2)), dma((2, LANES, 2)), dma((2, 2)), dma((2, 2)),
         ],
         compiler_params=pltpu.CompilerParams(
-            collective_id=0, has_side_effects=True, vmem_limit_bytes=63 * 1024 * 1024
+            collective_id=0, has_side_effects=True, vmem_limit_bytes=56 * 1024 * 1024
         ),
     )(
         jnp.transpose(distribution, (1, 0, 2)), freestream, face_area, cell_volume.reshape(1, CELLS), neighbours,

time: 45.9 us -> 43.7 us (0.952)
  Pallas kernels: 43.9 us -> 42.6 us
  local copies, waits for them, and re-layouts: 1.8 us -> 0.76 us
    pallas_call x1, Pallas kernels: 43.9 us -> 42.6 us  [body(): pl.pallas_call(kernel, out_shape=pltpu.VMEM((PLANES, CELLS, FLAT), F32),...]
    unnamed x1, local copies, waits for them, and re-layouts: 1.8 us -> 0.76 us
where the time goes in v4:
time: 43.7 us; the launch traced here: 43.3 us
  Pallas kernels  42.6 us (97%)
  local copies, waits for them, and re-layouts  0.76 us (2%)
    pallas_call x1, Pallas kernels, body(): pl.pallas_call(kernel, out_shape=pltpu.VMEM((PLANES, CELLS, FLAT), F32),...  42.6 us

profile of v4, /device:TPU:1, one launch (start us, length us, event | category | flops | bytes accessed | tf_op | source)
XLA Modules:
  0.0 43.3 jit_solution(5245365442664917990)
XLA Ops:
  0.0 42.6 %shard_map.91 = f32[3,16,2304]{2,1,0:T(8,128)S(1)} custom-call(f32[3,16,2304]{2,1,0:T(8,128)} %bitcast.4, f32[3,2304]{1,0:T(4,128)} %free_h.1, f32[3,6,16]{2,1,0:T(8,128)} %area_h.1, f32[1,16]{1,0:T(1,128)} %bitcast.5, s32[6,16]{1,0:T(8,128)} %nb_h.1, s32[6,16]{1,0:T(8,128)} %wall_h.1, s32[2,4]{1,0:T(2,128)} %send_h.1, ...), custom_call_target="tpu_custom_call" | custom-call | tf_op jit(solution)/shard_map/pallas_call | solution.py:705
  42.6 0.8 %copy.11 = f32[16,3,2304]{2,0,1:T(8,128)} copy(f32[16,3,2304]{2,0,1:T(8,128)S(1)} %bitcast.3) | data formatting | bytes 884736

commit v5 on v4

--- a/solution.py
+++ b/solution.py
@@ -26,13 +26,16 @@
 BF16 = jnp.bfloat16
 
 
-PLANE_SUMS = 22
-TIMES_X = (0, 1, 2, 6, 7, 9, 10, 12, 13, 15, 16, 18, 19, 20, 21)
-TIMES_XX = (0, 6, 9, 12, 15, 18, 19, 20, 21)
 X_FACE = tuple(range(18))
-SENT = tuple(range(PLANE_SUMS)) + TIMES_X + TIMES_XX + X_FACE
-AT_X, AT_XX, AT_FACE = 22, 37, 46
-MOMENTS = (0, AT_X, 1, 2, AT_XX, 3, 4, AT_X + 1, AT_X + 2, 5)
+SUMMED = (
+    ((0, 0), (0, 1), (1, 0), (2, 0), (0, 2), (3, 0), (4, 0), (1, 1), (2, 1), (5, 0))
+    + tuple((c, 0) for c in range(6, 22))
+    + tuple((c, 1) for c in (6, 7, 9, 10, 12, 13, 15, 16, 18, 19, 20, 21))
+    + tuple((c, 2) for c in (6, 9, 12, 15, 18, 19, 20, 21))
+)
+AT_FACE = len(SUMMED)
+SENT = tuple(c for c, _ in SUMMED) + X_FACE
+KINDS = tuple(power for _, power in SUMMED) + (3,) * len(X_FACE)
 
 
 def plane_sums(j, k):
@@ -68,7 +71,7 @@
 
     planes = plane_sums(at[1], at[2])
     x = velocity(at[0])
-    basis = [planes[c] for c in range(PLANE_SUMS)] + [planes[c] * x for c in TIMES_X] + [planes[c] * x * x for c in TIMES_XX]
+    basis = [planes[c] * x**power for c, power in SUMMED]
     for end in (0, NV - 1):
         basis += [planes[c] * (at[0] == end) for c in X_FACE]
 
@@ -104,15 +107,17 @@
     row = np.arange(128)[:, None]
     col = np.arange(1280)[None, :] // 128
     ratios = row // 16 == col[:, :768]
-    moments = row == np.array(MOMENTS)[col]
+    moments = row % 16 == col
     products = (row % 10 == col) & (row < 110)
     stencil = np.zeros((128, 128))
     stencil[:, :100] = stencil_moments()
-    for m, lane in enumerate(MOMENTS):
-        stencil[lane, 100 + m] = 1.0
+    for m in range(10):
+        stencil[m, 100 + m] = 1.0
     plain = [a.astype(jnp.bfloat16) for a in (ratios, moments, products)]
     whole = np.concatenate(plain + list(two_parts(stencil)), axis=1)
-    return np.concatenate(np.split(whole, whole.shape[1] // 128, axis=1), axis=0)
+    kinds = np.zeros((16, 128))
+    kinds[0:4] = np.arange(4)[:, None] == np.array(KINDS + KINDS)[None, :]
+    return np.concatenate(np.split(whole, whole.shape[1] // 128, axis=1) + [kinds.astype(jnp.bfloat16)], axis=0)
 
 
 def split2(x):
@@ -162,9 +167,9 @@
 def kernel(
     dist, free_h, area_h, vol_h, nb_h, wall_h, send_h, wts_h, mat_h, out,
     free, area, vol, nb, wall, send, distv, hs, hr, wts, mat, pb, fa, wb, fb, relay, qm, fq, pm,
-    yt, zt, mt, prm, sb, lhs, fsend, frecv, mrecv,
+    yt, zt, mt, prm, sb, lhs, fsend, frecv, asend, arecv, yrecv, zrecv,
     in_sem, h_ssem, h_rsem, f_ssem, f_rsem, m_ssem, m_rsem, p_ssem, p_rsem,
-    s_sem, z_ssem, z_rsem, r_ssem, r_rsem,
+    s_sem, z_ssem, z_rsem, r_ssem, r_rsem, b_ssem, b_rsem,
 ):
     space = lax.axis_index("space")
     vel = lax.axis_index("vel")
@@ -536,23 +541,39 @@
         acc.append(plane)
     acc = jnp.concatenate(acc, axis=0)
     acc = acc + pltpu.roll(acc, 64, 1)
-    lane = lax.broadcasted_iota(jnp.int32, (CELLS, 128), 1) & 63
+    kinds = mat[28 * 128 : 28 * 128 + 16, :].astype(F32)
     sent = None
     for p in range(PLANES):
-        face = 0.0
+        weight = kinds[0:1] + kinds[1:2] * xs[p] + kinds[2:3] * (xs[p] * xs[p])
         if p == 0:
-            face = jnp.where(has_left, 0.0, 1.0)
+            weight = weight + kinds[3:4] * jnp.where(has_left, 0.0, 1.0)
         if p == PLANES - 1:
-            face = jnp.where(has_right, 0.0, 1.0)
-        weight = jnp.where(
-            lane < AT_X, 1.0, jnp.where(lane < AT_XX, xs[p], jnp.where(lane < AT_FACE, xs[p] * xs[p], face))
-        )
+            weight = weight + kinds[3:4] * jnp.where(has_right, 0.0, 1.0)
         term = weight * acc[CELLS * p : CELLS * p + CELLS]
         sent = term if p == 0 else sent + term
-    low = lax.broadcasted_iota(jnp.int32, (8, 128), 1) < 64
-    mrecv[0] = jnp.where(low, sent[0:8], sent[8:16])
+
+    lane8 = lax.broadcasted_iota(jnp.int32, (8, 128), 1)
+    for half in range(2):
+        own = jnp.where(lane8 < 16, sent[8 * half : 8 * half + 8], 0.0)
+        asend[half : half + 1, :] = jnp.sum(pltpu.roll(own, 0, 1, stride=16, stride_axis=0), axis=0, keepdims=True)
     for d in FAR_FIRST:
-        gather_copy(mrecv.at[0], mrecv, m_ssem, m_rsem, d).start()
+        gather_copy(asend, arecv, m_ssem, m_rsem, d).start()
+
+    def along_copy(buf, k, d, to):
+        return pltpu.make_async_remote_copy(
+            src_ref=buf.at[0], dst_ref=buf.at[d], send_sem=b_ssem.at[k, d], recv_sem=b_rsem.at[k, d],
+            device_id=(space, to), device_id_type=MESH,
+        )
+
+    def y_copy(d):
+        return along_copy(yrecv, 0, d, z_at * LANES + lax.rem(y_at + d, LANES))
+
+    def z_copy(d):
+        return along_copy(zrecv, 1, d, lax.rem(z_at + d, LANES) * LANES + y_at)
+
+    yrecv[0] = jnp.where(lane8 < 64, sent[0:8], sent[8:16])
+    for d in (2, 1, 3):
+        y_copy(d).start()
 
     def add_walls(t, acc):
         off = pl.multiple_of(t * 128, 128)
@@ -573,23 +594,12 @@
         return acc
 
     pass_on()
+    for d in range(1, LANES):
+        y_copy(d).wait_recv()
+    zrecv[0] = (yrecv[0] + yrecv[1]) + (yrecv[2] + yrecv[3])
+    for d in (2, 1, 3):
+        z_copy(d).start()
     lax.fori_loop(0, FLAT // 128, halo_walls, 0, unroll=3)
-
-    for d in range(1, VELS):
-        gather_copy(mrecv.at[0], mrecv, m_ssem, m_rsem, d).wait_recv()
-    packed = mrecv[0]
-    for d in range(1, VELS):
-        packed = packed + mrecv[d]
-
-    def unpack(x):
-        return jnp.concatenate([x, pltpu.roll(x, 64, 1)], axis=0)
-
-    lane = lax.broadcasted_iota(jnp.int32, (CELLS, 128), 1)
-    on_face = (lane >= AT_FACE) & (lane < 64)
-    least = unpack(mrecv[vel])
-    largest = unpack(mrecv[lax.rem(vel + 1, VELS)])
-    sums = jnp.where(lane < AT_FACE, unpack(packed), jnp.where(on_face, least, 0.0))
-    sums = sums + pltpu.roll(jnp.where(on_face, largest, 0.0), len(X_FACE), 1)
 
     def coefficients(allm):
         m = [allm[:, 128 * i : 128 * i + 128] for i in range(10)]
@@ -607,12 +617,31 @@
             gxy=4.0 * a * cxy, gxz=4.0 * a * cxz, gyz=4.0 * a * cyz,
         )
 
-    terms, c1 = coefficients(times(sums, columns(mat, 6, 10)))
-    factor = jnp.where(lane < 110, 1.0, 0.0)
-    for t in range(10):
-        factor = jnp.where((lane >= 10 * t) & (lane < 10 * t + 10), terms[t], factor)
-    stencil = times(sums, columns(mat, 26, 2))
-    _, c2 = coefficients(times(factor * (stencil[:, 0:128] + stencil[:, 128:256]), columns(mat, 16, 10)))
+    lane = lax.broadcasted_iota(jnp.int32, (CELLS, 128), 1)
+    cell = lax.broadcasted_iota(jnp.int32, (CELLS, 128), 0)
+    moments = total(asend, arecv, m_ssem, m_rsem)
+    moments = jnp.concatenate([jnp.broadcast_to(moments[half : half + 1], (8, 128)) for half in range(2)], axis=0)
+    moments = jnp.where((lane >> 4) == (cell & 7), moments, 0.0)
+    terms, c1 = coefficients(times(moments, columns(mat, 6, 10)))
+
+    def second_coefficients():
+        for d in range(1, LANES):
+            z_copy(d).wait_recv()
+        packed = (zrecv[0] + zrecv[1]) + (zrecv[2] + zrecv[3])
+
+        def unpack(x):
+            return jnp.concatenate([x, pltpu.roll(x, 64, 1)], axis=0)
+
+        on_face = (lane >= AT_FACE) & (lane < 64)
+        least = unpack(zrecv[z_at])
+        largest = unpack(zrecv[lax.rem(z_at + 1, LANES)])
+        sums = jnp.where(lane < AT_FACE, unpack(packed), jnp.where(on_face, least, 0.0))
+        sums = sums + pltpu.roll(jnp.where(on_face, largest, 0.0), len(X_FACE), 1)
+        factor = jnp.where(lane < 110, 1.0, 0.0)
+        for t in range(10):
+            factor = jnp.where((lane >= 10 * t) & (lane < 10 * t + 10), terms[t], factor)
+        stencil = times(sums, columns(mat, 26, 2))
+        return coefficients(times(factor * (stencil[:, 0:128] + stencil[:, 128:256]), columns(mat, 16, 10)))[1]
 
     width = 768
 
@@ -660,6 +689,9 @@
 
     relax_plane(fa, 3, fb, 2, 1, c1)
 
+    def edge(right):
+        return jnp.where(right, PLANES + 1, 2)
+
     def relax_side(right):
         left = jnp.logical_not(right)
         recv_planes(True, left)
@@ -667,7 +699,6 @@
         arrived = jnp.where(right, PLANES + 2, 0)
         walls = jnp.where(right, 2, 0)
         halo_at = jnp.where(right, PLANES + 2, 1)
-        edge_at = jnp.where(right, PLANES + 1, 2)
 
         @pl.when((right & has_right) | (left & has_left))
         def _():
@@ -675,12 +706,18 @@
                 fa[arrived + i, :, MARGIN : MARGIN + FLAT] = fa[arrived + i, :, MARGIN : MARGIN + FLAT] + wb[walls + i]
             relax_plane(fa, halo_at, fb, halo_at - 1, halo_at - 2, c1)
 
-        relax_plane(fa, edge_at, fb, edge_at - 1, edge_at - 2, c1)
-        relax_plane(fb, edge_at - 1, out, edge_at - 2, edge_at - 2, c2)
+        relax_plane(fa, edge(right), fb, edge(right) - 1, edge(right) - 2, c1)
+
+    def relax_again(right):
+        relax_plane(fb, edge(right) - 1, out, edge(right) - 2, edge(right) - 2, c2)
 
     right_first = y_at == 0
+    right_last = jnp.logical_not(right_first)
     relax_side(right_first)
-    relax_side(jnp.logical_not(right_first))
+    c2 = second_coefficients()
+    relax_again(right_first)
+    relax_side(right_last)
+    relax_again(right_last)
     relax_plane(fb, 2, out, 1, 1, c2)
 
     @pl.when(has_above)
@@ -695,7 +732,10 @@
 
     for d in range(1, VELS):
         gather_copy(fsend, frecv, f_ssem, f_rsem, d).wait_send()
-        gather_copy(mrecv.at[0], mrecv, m_ssem, m_rsem, d).wait_send()
+        gather_copy(asend, arecv, m_ssem, m_rsem, d).wait_send()
+    for d in range(1, LANES):
+        y_copy(d).wait_send()
+        z_copy(d).wait_send()
     end_planes()
 
 
@@ -718,7 +758,7 @@
             pltpu.VMEM((2, PLANES, HALO, FLAT), F32),
             pltpu.VMEM((2, PLANES, HALO, FLAT), F32),
             pltpu.VMEM((FLAT, 128), BF16),
-            pltpu.VMEM((28 * 128, 128), BF16),
+            pltpu.VMEM((28 * 128 + 16, 128), BF16),
             pltpu.VMEM((PLANES, CELLS, FLAT), F32),
             pltpu.VMEM((PLANES + 4, CELLS, WIDE), F32),
             pltpu.VMEM((4, CELLS, FLAT), F32),
@@ -735,10 +775,14 @@
             pltpu.VMEM((96, 64), BF16),
             pltpu.VMEM((1, 256), F32),
             pltpu.VMEM((VELS, 1, 256), F32),
-            pltpu.VMEM((VELS, 8, 128), F32),
+            pltpu.VMEM((2, 128), F32),
+            pltpu.VMEM((VELS, 2, 128), F32),
+            pltpu.VMEM((LANES, 8, 128), F32),
+            pltpu.VMEM((LANES, 8, 128), F32),
             dma((PLANES,)), dma((2, PLANES)), dma((2, PLANES)),
             dma((VELS,)), dma((VELS,)), dma((VELS,)), dma((VELS,)), dma((2, 2)), dma((2, 2)),
             dma((8,)), dma((2, LANES, 2)), dma((2, LANES, 2)), dma((2, 2)), dma((2, 2)),
+            dma((2, LANES)), dma((2, LANES)),
         ],
         compiler_params=pltpu.CompilerParams(
             collective_id=0, has_side_effects=True, vmem_limit_bytes=56 * 1024 * 1024

time: 43.7 us -> 43.4 us (level)
  no operation moved by 1% of the time
where the time goes in v5:
time: 43.4 us; the launch traced here: 43.3 us
  Pallas kernels  42.5 us (98%)
  local copies, waits for them, and re-layouts  0.76 us (2%)
    pallas_call x1, Pallas kernels, body(): pl.pallas_call(kernel, out_shape=pltpu.VMEM((PLANES, CELLS, FLAT), F32),...  42.5 us

profile of v5, /device:TPU:1, one launch (start us, length us, event | category | flops | bytes accessed | tf_op | source)
XLA Modules:
  0.0 43.3 jit_solution(2804072265692432154)
XLA Ops:
  0.0 42.5 %shard_map.91 = f32[3,16,2304]{2,1,0:T(8,128)S(1)} custom-call(f32[3,16,2304]{2,1,0:T(8,128)} %bitcast.4, f32[3,2304]{1,0:T(4,128)} %free_h.1, f32[3,6,16]{2,1,0:T(8,128)} %area_h.1, f32[1,16]{1,0:T(1,128)} %bitcast.5, s32[6,16]{1,0:T(8,128)} %nb_h.1, s32[6,16]{1,0:T(8,128)} %wall_h.1, s32[2,4]{1,0:T(2,128)} %send_h.1, ...), custom_call_target="tpu_custom_call" | custom-call | tf_op jit(solution)/shard_map/pallas_call | solution.py:745
  42.5 0.8 %copy.11 = f32[16,3,2304]{2,0,1:T(8,128)} copy(f32[16,3,2304]{2,0,1:T(8,128)S(1)} %bitcast.3) | data formatting | bytes 884736

commit v6 on v5

--- a/solution.py
+++ b/solution.py
@@ -167,7 +167,7 @@
 def kernel(
     dist, free_h, area_h, vol_h, nb_h, wall_h, send_h, wts_h, mat_h, out,
     free, area, vol, nb, wall, send, distv, hs, hr, wts, mat, pb, fa, wb, fb, relay, qm, fq, pm,
-    yt, zt, mt, prm, sb, lhs, fsend, frecv, asend, arecv, yrecv, zrecv,
+    yt, zt, mt, kt, lf, prm, sb, lhs, fsend, frecv, asend, arecv, yrecv, zrecv,
     in_sem, h_ssem, h_rsem, f_ssem, f_rsem, m_ssem, m_rsem, p_ssem, p_rsem,
     s_sem, z_ssem, z_rsem, r_ssem, r_rsem, b_ssem, b_rsem,
 ):
@@ -208,6 +208,9 @@
     z = (flat - row * NV - (NV - 1) / 2.0) * STEP
     yt[...] = y
     zt[...] = z
+    last_z = (NV - 1) / 2.0 * STEP - 0.1
+    kt[0] = jnp.where(z < last_z, 1.0, 0.0)
+    kt[1] = jnp.where(z > -last_z, 1.0, 0.0)
     mt[...] = jnp.exp(-(y * y + z * z) / 2.0)
     for buf, count in ((fa, PLANES + 4), (fb, PLANES + 2)):
         for plane in range(count):
@@ -394,17 +397,22 @@
             device_id=(space, (z_at + dz) * LANES + other), device_id_type=MESH,
         )
 
-    def send_plane(right, n):
+    def send_far(right, n):
         home, _, _, inner = sides(right)
-
-        @pl.when(y_at != home)
-        def _():
-            near_copy(right, n).start()
 
         @pl.when((y_at == home) & inner)
         def _():
             for q in range(LANES):
                 part_copy(right, n, q).start()
+
+    def send_near():
+        for right in (True, False):
+            home, _, _, _ = sides(right)
+
+            @pl.when(y_at != home)
+            def _():
+                for n in range(2):
+                    near_copy(right, n).start()
 
     def pass_on():
         for step in range(2):
@@ -500,17 +508,17 @@
 
         flow_plane(p)
         if step == 0:
-            send_plane(True, 0)
-            send_plane(False, 1)
+            send_far(True, 0)
+            send_far(False, 1)
         else:
 
             @pl.when(p == PLANES - 1)
             def _():
-                send_plane(True, 1)
+                send_far(True, 1)
 
             @pl.when(p == 0)
             def _():
-                send_plane(False, 0)
+                send_far(False, 0)
 
     rows = PLANES * CELLS
     flow = jnp.dot(pm[...], wts[...], preferred_element_type=F32)
@@ -574,6 +582,7 @@
     yrecv[0] = jnp.where(lane8 < 64, sent[0:8], sent[8:16])
     for d in (2, 1, 3):
         y_copy(d).start()
+    send_near()
 
     def add_walls(t, acc):
         off = pl.multiple_of(t * 128, 128)
@@ -643,17 +652,23 @@
         stencil = times(sums, columns(mat, 26, 2))
         return coefficients(times(factor * (stencil[:, 0:128] + stencil[:, 128:256]), columns(mat, 16, 10)))[1]
 
-    width = 768
-
-    def relax_plane(src, at, dst, dst_at, p, c):
+    width = FLAT
+
+    def lane_factors(k, c):
+        a2, a2uy, a2uz, zq = (rep(c[q], FLAT // 128) for q in ("a2", "a2uy", "a2uz", "zq"))
+        drift = a2 * zt[...] - a2uz
+        lf[k, 0] = a2 * yt[...] - a2uy
+        lf[k, 1] = zq + drift
+        lf[k, 2] = zq - drift
+
+    def relax_plane(src, at, dst, dst_at, p, c, k):
         n = width // 128
         margin = MARGIN if dst.shape[-1] == WIDE else 0
         x = x_of(p)
         drift_n = c["a2"] * (x + STEP - c["ux"]) + c["lx"]
         drift_p = c["lx"] - c["a2"] * (x - STEP - c["ux"])
         kn, kp, k0 = rep(drift_n, n), rep(drift_p, n), rep(c["k0"], n)
-        ys, a2, a2uy, a2uz, zq = (rep(c[q], n) for q in ("ys", "a2", "a2uy", "a2uz", "zq"))
-        gxy, gxz, gyz = (rep(c[q], n) for q in ("gxy", "gxz", "gyz"))
+        ys, gxy, gxz, gyz = (rep(c[q], n) for q in ("ys", "gxy", "gxz", "gyz"))
 
         def step(t, acc):
             off = pl.multiple_of(t * width, 128)
@@ -661,7 +676,6 @@
             cen = pl.ds(off, width)
             cw, nw, pw = src[at, :, win], src[at + 1, :, win], src[at - 1, :, win]
             xw = nw - pw
-            yy, zz = yt[:, cen], zt[:, cen]
             total_w = width + 2 * MARGIN
 
             def up(v):
@@ -674,20 +688,19 @@
             u, d = up(cw), down(cw)
             diff = u - d
             res = k0 * cc + kn * nn + kp * pp
-            res = res + ys * (u + d) + (a2 * yy - a2uy) * diff + gxy * (up(xw) - down(xw))
+            res = res + ys * (u + d) + lf[k, 0, :, cen] * diff + gxy * (up(xw) - down(xw))
             cross = gxz * (nn - pp) + gyz * diff
-            zr = a2 * zz - a2uz
-            plus = (zq + zr) * cc + cross
-            minus = (zq - zr) * cc - cross
-            edge = (NV - 1) / 2.0 * STEP
-            res = res + jnp.where(zz < edge - 0.1, pltpu.roll(plus, width - 1, 1), 0.0)
-            res = res + jnp.where(zz > 0.1 - edge, pltpu.roll(minus, 1, 1), 0.0)
+            plus = lf[k, 1, :, cen] * cc + cross
+            minus = lf[k, 2, :, cen] * cc - cross
+            res = res + kt[0, :, cen] * pltpu.roll(plus, width - 1, 1)
+            res = res + kt[1, :, cen] * pltpu.roll(minus, 1, 1)
             dst[dst_at, :, pl.ds(off + margin, width)] = res
             return acc
 
         lax.fori_loop(0, FLAT // width, step, 0, unroll=True)
 
-    relax_plane(fa, 3, fb, 2, 1, c1)
+    lane_factors(0, c1)
+    relax_plane(fa, 3, fb, 2, 1, c1, 0)
 
     def edge(right):
         return jnp.where(right, PLANES + 1, 2)
@@ -704,21 +717,22 @@
         def _():
             for i in range(2):
                 fa[arrived + i, :, MARGIN : MARGIN + FLAT] = fa[arrived + i, :, MARGIN : MARGIN + FLAT] + wb[walls + i]
-            relax_plane(fa, halo_at, fb, halo_at - 1, halo_at - 2, c1)
-
-        relax_plane(fa, edge(right), fb, edge(right) - 1, edge(right) - 2, c1)
+            relax_plane(fa, halo_at, fb, halo_at - 1, halo_at - 2, c1, 0)
+
+        relax_plane(fa, edge(right), fb, edge(right) - 1, edge(right) - 2, c1, 0)
 
     def relax_again(right):
-        relax_plane(fb, edge(right) - 1, out, edge(right) - 2, edge(right) - 2, c2)
+        relax_plane(fb, edge(right) - 1, out, edge(right) - 2, edge(right) - 2, c2, 1)
 
     right_first = y_at == 0
     right_last = jnp.logical_not(right_first)
     relax_side(right_first)
     c2 = second_coefficients()
+    lane_factors(1, c2)
     relax_again(right_first)
     relax_side(right_last)
     relax_again(right_last)
-    relax_plane(fb, 2, out, 1, 1, c2)
+    relax_plane(fb, 2, out, 1, 1, c2, 1)
 
     @pl.when(has_above)
     def _():
@@ -770,6 +784,8 @@
             pltpu.VMEM((CELLS, FLAT), F32),
             pltpu.VMEM((CELLS, FLAT), F32),
             pltpu.VMEM((CELLS, FLAT), F32),
+            pltpu.VMEM((2, CELLS, FLAT), F32),
+            pltpu.VMEM((2, 3, CELLS, FLAT), F32),
             pltpu.VMEM((32, 128), F32),
             pltpu.VMEM((32, CELLS, 128), F32),
             pltpu.VMEM((96, 64), BF16),

time: 43.4 us -> 42.5 us (0.979)
  Pallas kernels: 42.5 us -> 41.5 us
    pallas_call x1, Pallas kernels: 42.5 us -> 41.5 us  [body(): pl.pallas_call(kernel, out_shape=pltpu.VMEM((PLANES, CELLS, FLAT), F32),...]
where the time goes in v6:
time: 42.5 us; the launch traced here: 42.3 us
  Pallas kernels  41.5 us (98%)
  local copies, waits for them, and re-layouts  0.76 us (2%)
    pallas_call x1, Pallas kernels, body(): pl.pallas_call(kernel, out_shape=pltpu.VMEM((PLANES, CELLS, FLAT), F32),...  41.5 us

profile of v6, /device:TPU:1, one launch (start us, length us, event | category | flops | bytes accessed | tf_op | source)
XLA Modules:
  0.0 42.3 jit_solution(6756116600303164718)
XLA Ops:
  0.0 41.5 %shard_map.91 = f32[3,16,2304]{2,1,0:T(8,128)S(1)} custom-call(f32[3,16,2304]{2,1,0:T(8,128)} %bitcast.4, f32[3,2304]{1,0:T(4,128)} %free_h.1, f32[3,6,16]{2,1,0:T(8,128)} %area_h.1, f32[1,16]{1,0:T(1,128)} %bitcast.5, s32[6,16]{1,0:T(8,128)} %nb_h.1, s32[6,16]{1,0:T(8,128)} %wall_h.1, s32[2,4]{1,0:T(2,128)} %send_h.1, ...), custom_call_target="tpu_custom_call" | custom-call | tf_op jit(solution)/shard_map/pallas_call | solution.py:759
  41.5 0.8 %copy.11 = f32[16,3,2304]{2,0,1:T(8,128)} copy(f32[16,3,2304]{2,0,1:T(8,128)S(1)} %bitcast.3) | data formatting | bytes 884736

commit v7 on v6

--- a/solution.py
+++ b/solution.py
@@ -308,6 +308,9 @@
     y_at, z_at = lax.rem(vel, LANES), vel // LANES
     first = jnp.where(y_at == LANES - 1, PLANES - 1, 0)
     order = (1, first, PLANES - 1 - first)
+    for d in FAR_FIRST:
+        gather_copy(fsend, frecv, f_ssem, f_rsem, d).start()
+
     for p in order:
 
         @pl.when(has_above)
@@ -327,9 +330,6 @@
     def _():
         for p in range(PLANES):
             hr[1, p] = jnp.broadcast_to(free[p : p + 1, :], (HALO, FLAT))
-
-    for d in FAR_FIRST:
-        gather_copy(fsend, frecv, f_ssem, f_rsem, d).start()
 
     for copy in late:
         copy.wait()
@@ -402,7 +402,7 @@
 
         @pl.when((y_at == home) & inner)
         def _():
-            for q in range(LANES):
+            for q in sorted(range(LANES), key=lambda q: q == home):
                 part_copy(right, n, q).start()
 
     def send_near():
@@ -582,7 +582,6 @@
     yrecv[0] = jnp.where(lane8 < 64, sent[0:8], sent[8:16])
     for d in (2, 1, 3):
         y_copy(d).start()
-    send_near()
 
     def add_walls(t, acc):
         off = pl.multiple_of(t * 128, 128)
@@ -591,7 +590,6 @@
             fa[p + 2, :, pl.ds(off + MARGIN, 128)] = pb[p, :, pl.ds(off, 128)] + walls[p]
         return acc
 
-    lax.fori_loop(0, FLAT // 128, add_walls, 0, unroll=3)
 
     halo_planes = (-2, -1, PLANES, PLANES + 1)
 
@@ -603,11 +601,13 @@
         return acc
 
     pass_on()
+    send_near()
     for d in range(1, LANES):
         y_copy(d).wait_recv()
     zrecv[0] = (yrecv[0] + yrecv[1]) + (yrecv[2] + yrecv[3])
     for d in (2, 1, 3):
         z_copy(d).start()
+    lax.fori_loop(0, FLAT // 128, add_walls, 0, unroll=3)
     lax.fori_loop(0, FLAT // 128, halo_walls, 0, unroll=3)
 
     def coefficients(allm):
@@ -727,10 +727,10 @@
     right_first = y_at == 0
     right_last = jnp.logical_not(right_first)
     relax_side(right_first)
+    relax_side(right_last)
     c2 = second_coefficients()
     lane_factors(1, c2)
     relax_again(right_first)
-    relax_side(right_last)
     relax_again(right_last)
     relax_plane(fb, 2, out, 1, 1, c2, 1)
 

time: 42.5 us -> 42.3 us (level)
  no operation moved by 1% of the time
where the time goes in v7:
time: 42.3 us; the launch traced here: 42 us
  Pallas kernels  41.2 us (97%)
  local copies, waits for them, and re-layouts  0.76 us (2%)
    pallas_call x1, Pallas kernels, body(): pl.pallas_call(kernel, out_shape=pltpu.VMEM((PLANES, CELLS, FLAT), F32),...  41.2 us

profile of v7, /device:TPU:1, one launch (start us, length us, event | category | flops | bytes accessed | tf_op | source)
XLA Modules:
  0.0 42.0 jit_solution(5119571721836981005)
XLA Ops:
  0.0 41.2 %shard_map.91 = f32[3,16,2304]{2,1,0:T(8,128)S(1)} custom-call(f32[3,16,2304]{2,1,0:T(8,128)} %bitcast.4, f32[3,2304]{1,0:T(4,128)} %free_h.1, f32[3,6,16]{2,1,0:T(8,128)} %area_h.1, f32[1,16]{1,0:T(1,128)} %bitcast.5, s32[6,16]{1,0:T(8,128)} %nb_h.1, s32[6,16]{1,0:T(8,128)} %wall_h.1, s32[2,4]{1,0:T(2,128)} %send_h.1, ...), custom_call_target="tpu_custom_call" | custom-call | tf_op jit(solution)/shard_map/pallas_call | solution.py:759
  41.2 0.8 %copy.11 = f32[16,3,2304]{2,0,1:T(8,128)} copy(f32[16,3,2304]{2,0,1:T(8,128)S(1)} %bitcast.3) | data formatting | bytes 884736

commit v8 on v7

--- a/solution.py
+++ b/solution.py
@@ -177,6 +177,18 @@
     has_below, has_above = space > 0, space < blocks - 1
     has_left, has_right = vel > 0, vel < VELS - 1
 
+    barrier = pltpu.get_barrier_semaphore()
+    for d in FAR_FIRST:
+        pl.semaphore_signal(barrier, 1, device_id=(space, lax.rem(vel + d, VELS)), device_id_type=MESH)
+
+    @pl.when(has_below)
+    def _():
+        pl.semaphore_signal(barrier, 1, device_id=(space - 1, vel), device_id_type=MESH)
+
+    @pl.when(has_above)
+    def _():
+        pl.semaphore_signal(barrier, 1, device_id=(space + 1, vel), device_id_type=MESH)
+
     loads = [pltpu.make_async_copy(dist.at[p], distv.at[p], in_sem.at[p]) for p in range(PLANES)]
     small = [
         pltpu.make_async_copy(src, dst, s_sem.at[i])
@@ -189,18 +201,6 @@
     ]
     for copy in small + loads + late:
         copy.start()
-
-    barrier = pltpu.get_barrier_semaphore()
-    for d in FAR_FIRST:
-        pl.semaphore_signal(barrier, 1, device_id=(space, lax.rem(vel + d, VELS)), device_id_type=MESH)
-
-    @pl.when(has_below)
-    def _():
-        pl.semaphore_signal(barrier, 1, device_id=(space - 1, vel), device_id_type=MESH)
-
-    @pl.when(has_above)
-    def _():
-        pl.semaphore_signal(barrier, 1, device_id=(space + 1, vel), device_id_type=MESH)
 
     flat = lax.broadcasted_iota(jnp.int32, (CELLS, FLAT), 1).astype(F32)
     row = jnp.floor((flat + 0.5) / NV)

time: 42.3 us -> 42.3 us (level)
  no operation moved by 1% of the time
where the time goes in v8:
time: 42.3 us; the launch traced here: 42 us
  Pallas kernels  41.2 us (97%)
  local copies, waits for them, and re-layouts  0.76 us (2%)
    pallas_call x1, Pallas kernels, body(): pl.pallas_call(kernel, out_shape=pltpu.VMEM((PLANES, CELLS, FLAT), F32),...  41.2 us

profile of v8, /device:TPU:1, one launch (start us, length us, event | category | flops | bytes accessed | tf_op | source)
XLA Modules:
  0.0 42.0 jit_solution(2437911605674515675)
XLA Ops:
  0.0 41.2 %shard_map.91 = f32[3,16,2304]{2,1,0:T(8,128)S(1)} custom-call(f32[3,16,2304]{2,1,0:T(8,128)} %bitcast.4, f32[3,2304]{1,0:T(4,128)} %free_h.1, f32[3,6,16]{2,1,0:T(8,128)} %area_h.1, f32[1,16]{1,0:T(1,128)} %bitcast.5, s32[6,16]{1,0:T(8,128)} %nb_h.1, s32[6,16]{1,0:T(8,128)} %wall_h.1, s32[2,4]{1,0:T(2,128)} %send_h.1, ...), custom_call_target="tpu_custom_call" | custom-call | tf_op jit(solution)/shard_map/pallas_call | solution.py:759
  41.2 0.8 %copy.11 = f32[16,3,2304]{2,0,1:T(8,128)} copy(f32[16,3,2304]{2,0,1:T(8,128)S(1)} %bitcast.3) | data formatting | bytes 884736
